TPU v7x, 1024 devices: a whole 4x4x32 slice. The times are simulated.
1024 devices in a mesh: region: 64 (over z_lo, x), member: 16 (over z_hi, y, core).
Axes of the slice: x: 4, y: 4, z: 32 (z_hi: 2, z_lo: 16; z = z_hi * 16 + z_lo), core: 2. Of those that a mesh axis runs over, the one named last changes fastest.
Arguments:
- members: float32 [256, 1024, 1024], P('member', 'region'), may hold values from -6 to 6
- obs_value: float32 [1024, 1024], P('region'), may hold values from -6 to 6
- obs_precision: float32 [1024, 1024], P('region'), may hold values from 0.02 to 200
- obs_index: int32 [1024, 1024], P('region'), may hold values from 0 to 1023, as said below
- obs_count: int32 [1024], P('region'), may hold values from 256 to 1024
Outputs:
- analysis: float32 [256, 1024, 1024], P('member', 'region')
Inputs may be any that keep to these rules, and one draw needn't show every extreme that they name: `obs_count`: slots of a tile from its count onward are empty. `obs_index`: position within its own tile.
All inputs are finite; a program needn't handle non-finite values.
Results may differ from a plain program's by a relative error of at most 0.0005.
Values sent between devices are 32-bit elements; how exact they have to be, the bound alone decides.
No kernel may reach another device: no remote copies, remote signals or barrier semaphores. Data moves between devices by JAX's collectives and lax.ppermute only.
A program may use at most 32 MiB of HBM per device.

v0:
```python
import math

import jax
import jax.numpy as jnp
from jax import lax
from jax.sharding import Mesh
from jax.sharding import PartitionSpec as P

K = 256
ITERS = 12
MEMBER = ("member_0", "member_1", "member_2")


def in_blocks(x, dim, devices):
    before, after = (x.shape[:dim], x.shape[dim + 1 :])
    return jnp.moveaxis(x.reshape(*before, devices, -1, *after), dim, 0)


def in_order(parts, dim):
    parts = jnp.moveaxis(parts, 0, dim)
    shape = parts.shape
    return parts.reshape(*shape[:dim], shape[dim] * shape[dim + 1], *shape[dim + 2 :])


def moved_by_axis(parts, axes, turns):
    shape = [lax.axis_size(a) for a in axes]
    parts = parts.reshape(*shape, *parts.shape[1:])
    for k in turns:
        parts = lax.all_to_all(parts, axes[k], split_axis=k, concat_axis=k, tiled=True)
    return parts.reshape(-1, *parts.shape[len(axes) :])


def core_and_chips(x, groups, turns, split_dim, concat_dim):
    devices = lax.axis_size(groups[0]) * lax.axis_size(groups[1])
    parts = in_blocks(x, split_dim, devices)
    return in_order(moved_by_axis(parts, groups, turns), concat_dim)


def extended(block, sides, width):
    for axis, dim in sides:
        count = lax.axis_size(axis)
        forward = [(i, i + 1) for i in range(count - 1)]
        forward.append((count - 1, 0))
        backward = [(target, source) for source, target in forward]
        low = lax.ppermute(
            lax.slice_in_dim(block, block.shape[dim] - width, None, axis=dim), axis, forward
        )
        high = lax.ppermute(lax.slice_in_dim(block, 0, width, axis=dim), axis, backward)
        block = jnp.concatenate([low, block, high], axis=dim)
    return block


def observe(states, places, observed, accuracy, filled):
    average = jnp.sum(states, axis=0) / K
    deviation = states - average[None]
    sampled = jnp.take_along_axis(deviation, places[None], axis=2)
    baseline = jnp.take_along_axis(average, places, axis=1)
    slot_ids = jnp.arange(places.shape[1], dtype=jnp.int32)
    active = slot_ids[None, :] < filled[:, None]
    weight_root = jnp.where(active, jnp.sqrt(accuracy), jnp.float32(0.0))
    scaled = sampled * weight_root[None]
    innov_row = (weight_root * (observed - baseline))[None]
    stacked = jnp.concatenate([scaled, innov_row], axis=0)
    return (average, deviation, stacked)


def outer_gram(stacked):
    return jnp.einsum("ibo,jbo->bij", stacked, stacked, precision=lax.Precision.HIGHEST)


def transform_weights(gram_matrix):
    ensemble = gram_matrix.shape[1] - 1
    identity = jnp.eye(ensemble, dtype=jnp.float32)
    system = (ensemble - 1.0) * identity + gram_matrix[:, :ensemble, :ensemble]
    right_side = gram_matrix[:, :ensemble, ensemble]
    factor = jnp.sqrt(jnp.sum(system * system, axis=(1, 2)) + 1e-06)
    root_iter = system / factor[:, None, None]
    inverse_iter = jnp.broadcast_to(identity, system.shape)

    def one_sweep(sweep_no, iterates):
        root_now, inverse_now = iterates
        middle = 3.0 * identity - jnp.einsum(
            "bij,bjk->bik", inverse_now, root_now, precision=lax.Precision.HIGHEST
        )
        root_next = 0.5 * jnp.einsum(
            "bij,bjk->bik", root_now, middle, precision=lax.Precision.HIGHEST
        )
        inverse_next = 0.5 * jnp.einsum(
            "bij,bjk->bik", middle, inverse_now, precision=lax.Precision.HIGHEST
        )
        return (root_next, inverse_next)

    root_iter, inverse_iter = lax.fori_loop(0, ITERS, one_sweep, (root_iter, inverse_iter))
    inverse_root = inverse_iter / jnp.sqrt(factor)[:, None, None]
    pulled = jnp.einsum("bij,bj->bi", inverse_root, right_side, precision=lax.Precision.HIGHEST)
    shifted = jnp.einsum("bij,bj->bi", inverse_root, pulled, precision=lax.Precision.HIGHEST)
    return math.sqrt(ensemble - 1.0) * inverse_root + shifted[:, :, None]


def analyse(average, deviation, gram_matrix):
    weights = transform_weights(gram_matrix)
    return average[None] + jnp.einsum(
        "jbc,bjk->kbc", deviation, weights, precision=lax.Precision.HIGHEST
    )


def shards(members, obs_value, obs_precision, obs_index, obs_count):
    owned = members.shape[1] // lax.axis_size(MEMBER)
    first_band = lax.axis_index(MEMBER) * owned
    gathered_states = core_and_chips(members, (("member_0", "member_1"), "member_2"), (0, 1), 1, 0)

    def own_rows(tables):
        return lax.dynamic_slice_in_dim(tables, first_band, owned, 0)

    average, deviation, stacked = observe(
        gathered_states,
        own_rows(obs_index),
        own_rows(obs_value),
        own_rows(obs_precision),
        own_rows(obs_count),
    )
    beside_all = extended(outer_gram(stacked)[None], (("region", 0),), 1)
    gram_matrix = beside_all[1] + 0.5 * (beside_all[0] + beside_all[2])
    result = analyse(average, deviation, gram_matrix)
    return lax.all_to_all(result, MEMBER, split_axis=0, concat_axis=1, tiled=True)


def solution(mesh):
    split = Mesh(
        mesh.devices.reshape(mesh.shape["region"], 2, 4, 2),
        ("region", "member_0", "member_1", "member_2"),
    )
    placed = (
        P(MEMBER, "region", None),
        P("region", None),
        P("region", None),
        P("region", None),
        P("region"),
    )
    return jax.shard_map(
        shards, mesh=split, in_specs=placed, out_specs=P(MEMBER, "region", None), check_vma=False
    )
```

profile of v0, /device:TPU:121, one launch (start us, length us, event | category | flops | bytes accessed | tf_op | source)
XLA Modules:
  0.0 305.5 jit_solution(7106698037586695276)
XLA Ops:
  0.0 2.8 copy.14
  2.8 28.1 %all-to-all-start = ((f32[8,2,16,1,1024]{4,2,1,3,0:T(8,128)}), f32[8,2,16,1,1024]{4,2,1,3,0:T(8,128)S(1)}, u32[]{:S(2)}, u32[]{:S(2)}) async-start(f32[8,2,16,1,1024]{4,2,1,3,0:T(8,128)} %bitcast.2), calls=%async_computation | async-start | bytes 2097152 | tf_op jit(solution)/shard_map/all_to_all | solution.py:29
  30.9 0.6 dynamic_slice.13
  31.5 0.8 compare_select_fusion.1
  32.3 102.3 %all-to-all-done = f32[8,2,16,1,1024]{4,2,1,3,0:T(8,128)S(1)} async-done(((f32[8,2,16,1,1024]{4,2,1,3,0:T(8,128)}), f32[8,2,16,1,1024]{4,2,1,3,0:T(8,128)S(1)}, u32[]{:S(2)}, u32[]{:S(2)}) %all-to-all-start) | async-done | bytes 1048608 | tf_op jit(solution)/shard_map/all_to_all | solution.py:29
  134.7 6.0 %all_to_all.28 = f32[8,2,16,1,1024]{4,2,0,3,1:T(8,128)S(1)} all-to-all(f32[8,2,16,1,1024]{4,2,0,3,1:T(8,128)S(1)} %copy.15), channel_id=1, replica_groups=mesh['region'=64,'member_0'=2,'member_1'=4,'member_2'=2] {'member_2'}, dimensions={1} | all-to-all | bytes 2097152 | tf_op jit(solution)/shard_map/all_to_all | solution.py:29
  140.8 4.5 %gather_fusion.1 = f32[1024]{0:T(1024)S(1)} fusion(f32[1024]{0:T(1024)S(1)} %broadcast_multiply_fusion, s32[1024]{0:T(1024)S(1)} %broadcast_clamp_fusion), kind=kCustom, calls=%fused_computation.1 | custom fusion | bytes 12288 | tf_op jit(solution)/shard_map/jit(take_along_axis)/gather | solution.py:57
  145.6 1.3 copy.17
  146.9 1.4 subtract_bitcast_fusion
  148.3 1.4 multiply_bitcast_fusion
  149.7 1.0 copy.18
  150.7 3.5 %gather_fusion = f32[1024,256]{1,0:T(8,128)S(1)} fusion(f32[256,1024]{0,1:T(8,128)S(1)} %subtract_bitcast_fusion, s32[1024]{0:T(1024)S(1)} %broadcast_clamp_fusion.1), kind=kCustom, calls=%fused_computation | custom fusion | bytes 2101248 | tf_op jit(solution)/shard_map/jit(take_along_axis)/gather | solution.py:56
  154.5 0.7 copy-done
  155.2 3.2 %fusion.8 = f32[257,257]{0,1:T(8,128)S(1)} fusion(f32[1,1,1024]{0,2,1:T(8,128)S(1)} %copy-done, f32[256,1,1024]{0,2,1:T(8,128)S(1)} %fusion.12), kind=kOutput, calls=%fused_computation.14 | convolution fusion | flops 811873280 | bytes 1316868 | tf_op jit(solution)/shard_map/ibo,jbo->bij/dot_general | solution.py:68
  158.4 3.1 %collective-permute-start = (f32[1,1,257,257]{2,3,1,0:T(8,128)S(1)}, f32[1,1,257,257]{2,3,1,0:T(8,128)S(1)}, u32[]{:S(2)}, u32[]{:S(2)}) collective-permute-start(f32[1,1,257,257]{2,3,1,0:T(8,128)S(1)} %bitcast.98), channel_id=1, source_target_pairs={{0,16},{16,32},{32,48},{48,64},{64,80},{80,96},{96,112},{112,128},... | collective-permute-start | bytes 792596 | tf_op jit(solution)/shard_map/ppermute | solution.py:45
  161.6 4.3 %collective-permute-start.1 = (f32[1,1,257,257]{2,3,1,0:T(8,128)S(1)}, f32[1,1,257,257]{2,3,1,0:T(8,128)S(1)}, u32[]{:S(2)}, u32[]{:S(2)}) collective-permute-start(f32[1,1,257,257]{2,3,1,0:T(8,128)S(1)} %bitcast.99), channel_id=1, source_target_pairs={{16,0},{32,16},{48,32},{64,48},{80,64},{96,80},{112,96},{128,112},... | collective-permute-start | bytes 792596 | tf_op jit(solution)/shard_map/ppermute | solution.py:48
  166.0 7.0 %collective-permute-done = f32[1,1,257,257]{2,3,1,0:T(8,128)S(1)} collective-permute-done((f32[1,1,257,257]{2,3,1,0:T(8,128)S(1)}, f32[1,1,257,257]{2,3,1,0:T(8,128)S(1)}, u32[]{:S(2)}, u32[]{:S(2)}) %collective-permute-start) | collective-permute-done | bytes 264228 | tf_op jit(solution)/shard_map/ppermute | solution.py:45
  173.0 0.9 collective-permute-done.1
  174.0 0.7 multiply_reduce_fusion
  175.4 17.8 %while.13 = (s32[]{:T(128)}, f32[1,256,256]{1,2,0:T(8,128)S(1)}, f32[1,256,256]{2,1,0:T(8,128)S(1)}, s32[]{:T(128)}) while((s32[]{:T(128)}, f32[1,256,256]{1,2,0:T(8,128)S(1)}, f32[1,256,256]{2,1,0:T(8,128)S(1)}, s32[]{:T(128)}) %tuple.27), condition=%wide.region_3.4_spmd.clone, body=%wide.region_2.3_spmd.clone.sunk | while | flops 604307456 | bytes 3407925 | solution.py:93
  175.5 0.4 convolution_subtract_fusion.2
  176.3 0.6 fusion.46
  176.9 0.4 convolution_subtract_fusion.2
  177.8 0.6 fusion.46
  178.4 0.4 convolution_subtract_fusion.2
  179.2 0.6 fusion.46
  179.9 0.4 convolution_subtract_fusion.2
  180.7 0.6 fusion.46
  181.4 0.4 convolution_subtract_fusion.2
  182.2 0.6 fusion.46
  182.9 0.4 convolution_subtract_fusion.2
  183.7 0.6 fusion.46
  184.4 0.4 convolution_subtract_fusion.2
  185.2 0.6 fusion.46
  185.8 0.4 convolution_subtract_fusion.2
  186.6 0.6 fusion.46
  187.3 0.4 convolution_subtract_fusion.2
  188.1 0.6 fusion.46
  188.8 0.4 convolution_subtract_fusion.2
  189.6 0.6 fusion.46
  190.3 0.4 convolution_subtract_fusion.2
  191.1 0.6 fusion.46
  191.8 0.4 convolution_subtract_fusion.2
  192.6 0.6 fusion.46
  193.8 1.2 fusion.11
  195.0 1.1 copy.21
  196.1 107.9 %all_to_all.29 = f32[256,1,1024]{2,1,0:T(1,128)S(1)} all-to-all(f32[256,1,1024]{2,1,0:T(1,128)S(1)} %copy.21), channel_id=1, replica_groups=mesh['region'=64,'member_0'=2,'member_1'=4,'member_2'=2] {'member_0','me..., dimensions={0} | all-to-all | bytes 2097152 | tf_op jit(solution)/shard_map/all_to_all | solution.py:125
  304.0 1.6 copy.26
  (54 shorter events, 6.7 us)
Async XLA Ops:
  2.8 28.1 %copy-start.1 = (s32[16]{0:T(128)S(1)}, s32[16]{0:T(128)}, u32[]{:S(2)}) copy-start(s32[16]{0:T(128)} %param.11) | copy-start | bytes 196
  2.8 131.8 %all-to-all-start = ((f32[8,2,16,1,1024]{4,2,1,3,0:T(8,128)}), f32[8,2,16,1,1024]{4,2,1,3,0:T(8,128)S(1)}, u32[]{:S(2)}, u32[]{:S(2)}) async-start(f32[8,2,16,1,1024]{4,2,1,3,0:T(8,128)} %bitcast.2), calls=%async_computation | async-start | bytes 2097152 | tf_op jit(solution)/shard_map/all_to_all | solution.py:29
  154.2 1.0 copy-start
  158.4 14.6 %collective-permute-start = (f32[1,1,257,257]{2,3,1,0:T(8,128)S(1)}, f32[1,1,257,257]{2,3,1,0:T(8,128)S(1)}, u32[]{:S(2)}, u32[]{:S(2)}) collective-permute-start(f32[1,1,257,257]{2,3,1,0:T(8,128)S(1)} %bitcast.98), channel_id=1, source_target_pairs={{0,16},{16,32},{32,48},{48,64},{64,80},{80,96},{96,112},{112,128},... | collective-permute-start | bytes 792596 | tf_op jit(solution)/shard_map/ppermute | solution.py:45
  161.6 12.3 %collective-permute-start.1 = (f32[1,1,257,257]{2,3,1,0:T(8,128)S(1)}, f32[1,1,257,257]{2,3,1,0:T(8,128)S(1)}, u32[]{:S(2)}, u32[]{:S(2)}) collective-permute-start(f32[1,1,257,257]{2,3,1,0:T(8,128)S(1)} %bitcast.99), channel_id=1, source_target_pairs={{16,0},{32,16},{48,32},{64,48},{80,64},{96,80},{112,96},{128,112},... | collective-permute-start | bytes 792596 | tf_op jit(solution)/shard_map/ppermute | solution.py:48
where the time goes:
time: 306 us
  blocking collectives  114 us (37%)
  waiting for transfers between devices  110 us (36%)
  starting transfers between devices  35.5 us (12%)
  matrix products  21.7 us (7%)
  local copies, waits for them, and re-layouts  17.7 us (6%)
  other arithmetic  5.06 us (2%)
    all_to_all x1, blocking collectives, shards(): lax.all_to_all(result, MEMBER, split_axis=0, concat_axis=1, tiled=True)  108 us
    all_to_all x1, waiting for transfers between devices, moved_by_axis(): lax.all_to_all(parts, axes[k], split_axis=k, concat_axis=k, tiled=True)  102 us
    all_to_all x1, starting transfers between devices, moved_by_axis(): lax.all_to_all(parts, axes[k], split_axis=k, concat_axis=k, tiled=True)  28.1 us
    dot_general x12, matrix products, one_sweep(): jnp.einsum('bij,bjk->bik', root_now, middle, precision=lax.Precision.HIGH...  7.17 us
    ppermute x1, waiting for transfers between devices, extended(): lax.ppermute(lax.slice_in_dim(block, block.shape[dim] - width, None, axis...  7.02 us
  transfers between devices with their start and end apart: 3, of which 3 were waited for; matrix products, arithmetic and copies ran while one was open for 0% of the time, Pallas kernels for 0%

commit v1 on v0

v1 whole, which is shorter than its diff:
```python
import functools
import math

import jax
import jax.numpy as jnp
from jax import lax
from jax.experimental import pallas as pl
from jax.experimental.pallas import tpu as pltpu
from jax.sharding import Mesh
from jax.sharding import PartitionSpec as P

K = 256
ITERS = 12
HALF = K // 2
MEMBER = ("zh", "y", "core")
HIGHEST = lax.Precision.HIGHEST
VMEM = pl.BlockSpec(memory_space=pltpu.VMEM)
SMEM = pl.BlockSpec(memory_space=pltpu.SMEM)


def call(kernel, outs, specs, scratch=()):
    return pl.pallas_call(
        kernel,
        out_shape=outs,
        in_specs=specs,
        out_specs=jax.tree.map(lambda _: VMEM, outs),
        scratch_shapes=list(scratch),
        compiler_params=pltpu.CompilerParams(vmem_limit_bytes=24 << 20),
        cost_estimate=pl.CostEstimate(flops=0, bytes_accessed=0, transcendentals=0),
    )


def after(x, token):
    any_space = pl.BlockSpec(memory_space=pl.ANY)
    return pl.pallas_call(
        lambda token_ref, x_ref, out_ref: None,
        out_shape=f32(*x.shape),
        in_specs=[any_space] * 2,
        out_specs=any_space,
        input_output_aliases={1: 0},
    )(token, x)


def f32(*shape):
    return jax.ShapeDtypeStruct(shape, jnp.float32)


def split_kernel(zh_ref, x_ref, first_ref, own_ref, later_ref):
    def rows(band):
        return x_ref[:, band, :]

    for side in range(2):

        @pl.when(zh_ref[0] == side)
        def _():
            mine, theirs = 8 * side, 8 * (1 - side)
            for y in range(4):
                first_ref[pl.ds(16 * y, 16), :] = rows(theirs + 2 * y)
                later_ref[pl.ds(16 * y, 16), :] = rows(theirs + 2 * y + 1)
            for b in range(8):
                own_ref[pl.ds(16 * b, 16), :] = rows(mine + b)


def join_kernel(zh_ref, own_ref, back_ref, out_ref):
    for side in range(2):

        @pl.when(zh_ref[0] == side)
        def _():
            for b in range(8):
                out_ref[:, 8 * side + b, :] = own_ref[pl.ds(16 * b, 16), :]
                out_ref[:, 8 * (1 - side) + b, :] = back_ref[pl.ds(16 * b, 16), :]


def centred(own_ref, other_ref):
    states = jnp.concatenate([own_ref[...], other_ref[...]], axis=0)
    average = jnp.sum(states, axis=0, keepdims=True) / K
    return average, states - average


def product(a, b):
    return jnp.dot(a, b, precision=HIGHEST, preferred_element_type=jnp.float32)


def across(a, b):
    return lax.dot_general(
        a, b, (((1,), (1,)), ((), ())), precision=HIGHEST, preferred_element_type=jnp.float32
    )


def gram_kernel(on_ref, table_ref, own_ref, other_ref, gram_ref):
    @pl.when(on_ref[0] == 1)
    def _():
        average, deviation = centred(own_ref, other_ref)
        weight, pull = table_ref[0:1, :], table_ref[1:2, :]
        scaled = deviation * jnp.sqrt(weight)
        gram = across(scaled, scaled)
        right = across(jnp.broadcast_to(pull - weight * average, (8, 1024)), deviation)
        gram_ref[0:128, :] = gram[:HALF, :HALF]
        gram_ref[128:256, :] = gram[:HALF, HALF:]
        gram_ref[256:384, :] = gram[HALF:, HALF:]
        gram_ref[384:392, :] = right[:, :HALF]
        gram_ref[392:400, :] = right[:, HALF:]


def two_parts(x):
    high = x.astype(jnp.bfloat16)
    return high, (x - high.astype(jnp.float32)).astype(jnp.bfloat16)


def product3(a, b):
    (ah, al), (bh, bl) = two_parts(a), two_parts(b)
    dot = functools.partial(jnp.dot, preferred_element_type=jnp.float32)
    return dot(ah, bh) + (dot(ah, bl) + dot(al, bh))


def analyse_kernel(
    on_ref, gram_ref, west_ref, east_ref, own_ref, other_ref, mine_ref, theirs_ref, u_ref, z_ref
):
    @pl.when(on_ref[0] == 1)
    def _():
        total = gram_ref[...] + 0.5 * (west_ref[...] + east_ref[...])
        g11, g12, g22 = total[:128], total[128:256], total[256:384]
        right = jnp.concatenate([total[384:385], total[392:393]], axis=1)
        gram = jnp.concatenate(
            [jnp.concatenate([g11, g12], axis=1), jnp.concatenate([g12.T, g22], axis=1)], axis=0
        )
        rows = lax.broadcasted_iota(jnp.int32, (K, K), 0)
        columns = lax.broadcasted_iota(jnp.int32, (K, K), 1)
        diagonal = rows == columns
        system = gram + jnp.where(diagonal, K - 1.0, 0.0)
        factor = jnp.sqrt(jnp.sum(system * system, keepdims=True) + 1e-06)
        three = jnp.where(diagonal, 3.0, 0.0)
        root = system / factor
        middle = three - root
        u_ref[...] = 0.5 * product(root, middle)
        z_ref[...] = 0.5 * middle

        def sweep(_, carry):
            root, inverse = u_ref[...], z_ref[...]
            middle = three - product(inverse, root)
            u_ref[...] = 0.5 * product(root, middle)
            z_ref[...] = 0.5 * product(middle, inverse)
            return carry

        lax.fori_loop(0, ITERS - 2, sweep, 0)
        root, inverse = u_ref[...], z_ref[...]
        inverse = 0.5 * product(three - product(inverse, root), inverse)
        inverse = inverse / jnp.sqrt(factor)
        pulled = jnp.sum(inverse * right, axis=1, keepdims=True)
        shift = jnp.sum(inverse * pulled, axis=0, keepdims=True)
        weights = math.sqrt(K - 1.0) * inverse + shift
        average, deviation = centred(own_ref, other_ref)
        result = average + product3(weights, deviation)
        mine_ref[...] = result[:HALF]
        for part in range(8):
            core, y = part // 4, part % 4
            theirs_ref[pl.ds(16 * (2 * y + core), 16), :] = result[HALF + 16 * part : HALF + 16 * part + 16]


def shards(members, obs_value, obs_precision, obs_index, obs_count):
    zh, y, core = (lax.axis_index(a) for a in MEMBER)
    regions = lax.axis_size("region")
    width = members.shape[2]
    side = zh.astype(jnp.int32).reshape(1)
    on = [(core == s).astype(jnp.int32).reshape(1) for s in range(2)]

    first, own, later = call(
        split_kernel, (f32(64, width), f32(128, width), f32(64, width)), [SMEM, VMEM]
    )(side, members)

    def swap(x):
        return lax.ppermute(x, "zh", [(0, 1), (1, 0)])

    def swap_on(x, s):
        return lax.ppermute(x, ("zh", "core"), [(s, 2 + s), (2 + s, s)])

    def to_core(x, s):
        return lax.ppermute(x, "core", [(1 - s, s)])

    def over_y(x):
        return lax.all_to_all(x, "y", split_axis=0, concat_axis=0, tiled=True)

    def over_y_core(x):
        return lax.all_to_all(x, ("y", "core"), split_axis=0, concat_axis=0, tiled=True)

    def beside(x, s):
        found = []
        for odd in (0, 1):
            pairs = []
            for r in range(odd, regions, 2):
                ahead = (r + 1) % regions
                pairs += [(2 * r + s, 2 * ahead + s), (2 * ahead + s, 2 * r + s)]
            found.append(lax.ppermute(x, ("region", "core"), pairs))
        return found

    crossed = swap(first)
    always = obs_count[0] > 0

    def spread(later, own):
        near = over_y(later)
        far = to_core(near, 1)
        return jnp.concatenate([far, near]).reshape(HALF, width)

    def no_spread(later, own):
        return own.reshape(HALF, width)

    later = lax.cond(always, spread, no_spread, later, own)
    later_crossed = swap_on(later, 1)

    band = zh * 8 + y * 2 + core
    pick = lambda t: lax.dynamic_index_in_dim(t, band, 0, keepdims=False)
    places, observed, accuracy, filled = map(pick, (obs_index, obs_value, obs_precision, obs_count))
    slots = jnp.arange(width, dtype=jnp.int32)
    accuracy = jnp.where(slots < filled, accuracy, 0.0)
    hit = places[:, None] == slots[None, :]
    weight = jnp.sum(jnp.where(hit, accuracy[:, None], 0.0), axis=0)
    pull = jnp.sum(jnp.where(hit, (accuracy * observed)[:, None], 0.0), axis=0)
    table = jnp.stack([weight, pull])

    def analysed(s, own, table, other):
        gram = call(gram_kernel, f32(400, 128), [SMEM] + [VMEM] * 3)(
            on[s], table, own, other
        )
        west, east = beside(gram, s)
        return east, call(
            analyse_kernel,
            (f32(HALF, width), f32(HALF, width)),
            [SMEM] + [VMEM] * 5,
            scratch=[pltpu.VMEM((K, K), jnp.float32)] * 2,
        )(on[s], gram, west, east, own, other)

    def first_half(crossed, own, table):
        near = over_y(crossed)
        far = to_core(near, 0)
        return analysed(0, own, table, jnp.concatenate([near, far]).reshape(HALF, width))[1]

    def no_half(crossed, own, table):
        return jnp.zeros_like(own.reshape(HALF, width)), jnp.zeros_like(own.reshape(HALF, width))

    own = lax.cond(always, over_y_core, lambda x: x, own)
    crossed, own, table = lax.optimization_barrier((crossed, own, table))
    mine_0, theirs_0 = lax.cond(always, first_half, no_half, crossed, own, table)
    later_crossed, mine_0 = lax.optimization_barrier((later_crossed, mine_0))
    east, (mine_1, theirs_1) = analysed(1, own, table, later_crossed)
    pairs = [(2 * r + 1, 2 * r) for r in range(regions) if r % 4 in (0, 3)]
    gone = lax.ppermute(east[:8], ("region", "core"), pairs)
    theirs_0 = after(theirs_0, gone)
    back_0 = swap_on(theirs_0, 0)
    back_1 = swap_on(theirs_1, 1)
    mine = over_y_core(jnp.where(core == 0, mine_0, mine_1))
    back_0, mine = lax.optimization_barrier((back_0, mine))
    back = over_y_core(jnp.where(core == 0, back_0, back_1))
    return call(join_kernel, f32(*members.shape), [SMEM] + [VMEM] * 2)(side, mine, back)


def solution(mesh):
    split = Mesh(
        mesh.devices.reshape(mesh.shape["region"], 2, 4, 2), ("region", "zh", "y", "core")
    )
    placed = (
        P(MEMBER, "region", None),
        P("region", None),
        P("region", None),
        P("region", None),
        P("region"),
    )
    return jax.shard_map(
        shards, mesh=split, in_specs=placed, out_specs=P(MEMBER, "region", None), check_vma=False
    )
```

time: 306 us -> 279 us (0.912)
  the two profiles are of different devices: /device:TPU:121 before, /device:TPU:1 now
where the time goes in v1:
time: 279 us
  waiting for transfers between devices  137 us (49%)
  starting transfers between devices  62.4 us (22%)
  blocking collectives  56.6 us (20%)
  Pallas kernels  15.2 us (5%)
  local copies, waits for them, and re-layouts  3.33 us (1%)
    ppermute x3, waiting for transfers between devices, swap_on(): return lax.ppermute(x, ('zh', 'core'), [(s, 2 + s), (2 + s, s)])  118 us
    all_to_all x3, blocking collectives, over_y_core(): lax.all_to_all(x, ('y', 'core'), split_axis=0, concat_axis=0, tiled=True)  39.2 us
    ppermute x1, starting transfers between devices, swap(): return lax.ppermute(x, 'zh', [(0, 1), (1, 0)])  29.5 us
    all_to_all x2, blocking collectives, over_y(): return lax.all_to_all(x, 'y', split_axis=0, concat_axis=0, tiled=True)  17.4 us
    ppermute x3, starting transfers between devices, swap_on(): return lax.ppermute(x, ('zh', 'core'), [(s, 2 + s), (2 + s, s)])  15.2 us
    ppermute x4, waiting for transfers between devices, beside(): found.append(lax.ppermute(x, ('region', 'core'), pairs))  15.1 us
    pallas_call x2, Pallas kernels, analysed(): call(analyse_kernel, (f32(HALF, width), f32(HALF, width)), [SMEM] + [VMEM...  11.8 us
    ppermute x4, starting transfers between devices, beside(): found.append(lax.ppermute(x, ('region', 'core'), pairs))  11.1 us
  transfers between devices with their start and end apart: 11, of which 5 were waited for; matrix products, arithmetic and copies ran while one was open for 1% of the time, Pallas kernels for 4%

profile of v1, /device:TPU:1, one launch (start us, length us, event | category | flops | bytes accessed | tf_op | source)
XLA Modules:
  0.0 278.6 jit_solution(9014012851454035004)
XLA Ops:
  0.0 0.0 copy-start
  0.0 0.0 copy-start.3
  0.0 1.3 copy-done.1
  1.3 0.2 shard_map.55
  1.5 29.5 %collective-permute-start.4 = (f32[64,1024]{1,0:T(8,128)S(1)}, f32[64,1024]{1,0:T(8,128)S(1)}, u32[]{:S(2)}, u32[]{:S(2)}) collective-permute-start(f32[64,1024]{1,0:T(8,128)S(1)} %get-tuple-element.42), channel_id=1, source_target_pairs={{0,8},{8,0},{1,9},{9,1},{2,10},{10,2},{3,11},{11,3},{4,12},{12,4},... | collective-permute-start | bytes 786440 | tf_op jit(solution)/shard_map/ppermute | solution.py:172
  31.1 0.0 copy-done.3
  31.1 0.6 fusion.3
  32.3 15.0 %conditional.4 = (f32[128,1024]{1,0:T(8,128)}) conditional(s32[]{:T(128)} %bitcast.9, f32[128,1024]{1,0:T(8,128)S(1)} %get-tuple-element.43, f32[64,1024]{1,0:T(8,128)S(1)} %get-tuple-element.46), branch_computations={%region_4.5_spmd, %region_5.6_spmd} | conditional | flops 131072 | bytes 2621488 | solution.py:207
  32.4 9.5 %all_to_all.51 = f32[4,16,1024]{2,1,0:T(8,128)S(1)} all-to-all(f32[4,16,1024]{2,1,0:T(8,128)S(1)} %bitcast.31), channel_id=1, replica_groups=mesh['region'=64,'zh'=2,'y'=4,'core'=2] {'y'}, dimensions={0} | all-to-all | bytes 524288 | tf_op jit(solution)/shard_map/cond/branch_1_fun/all_to_all | solution.py:181
  41.9 1.3 collective-permute-start
  43.2 3.4 %collective-permute-done = f32[64,1024]{1,0:T(8,128)S(1)} collective-permute-done((f32[64,1024]{1,0:T(8,128)S(1)}, f32[64,1024]{1,0:T(8,128)S(1)}, u32[]{:S(2)}, u32[]{:S(2)}) %collective-permute-start) | collective-permute-done | bytes 262176 | tf_op jit(solution)/shard_map/cond/branch_1_fun/ppermute | solution.py:178
  46.5 0.8 pad_maximum_fusion
  47.4 5.7 %collective-permute-start.5 = (f32[128,1024]{1,0:T(8,128)}, f32[128,1024]{1,0:T(8,128)S(1)}, u32[]{:S(2)}, u32[]{:S(2)}) collective-permute-start(f32[128,1024]{1,0:T(8,128)} %get-tuple-element.69), channel_id=1, source_target_pairs={{1,9},{9,1},{3,11},{11,3},{5,13},{13,5},{7,15},{15,7},{17,25},{25,... | collective-permute-start | bytes 1572872 | tf_op jit(solution)/shard_map/ppermute | solution.py:175
  53.1 0.8 constant_dynamic-slice_fusion
  53.9 0.6 fusion.1
  54.5 11.8 %conditional.3 = (f32[128,1024]{1,0:T(8,128)S(1)}) conditional(s32[]{:T(128)} %bitcast.9, f32[128,1024]{1,0:T(8,128)S(1)} %get-tuple-element.43, f32[128,1024]{1,0:T(8,128)S(1)} %get-tuple-element.43), branch_computations={%region_0.0_spmd, %region_1.0_spmd} | conditional | bytes 2097160 | solution.py:240
  54.6 11.7 %all_to_all.50 = f32[8,16,1024]{2,1,0:T(8,128)S(1)} all-to-all(f32[8,16,1024]{2,1,0:T(8,128)S(1)} %copy.16), channel_id=1, replica_groups=mesh['region'=64,'zh'=2,'y'=4,'core'=2] {'y','core'}, dimensions={0} | all-to-all | bytes 1048576 | tf_op jit(solution)/shard_map/cond/branch_1_fun/all_to_all | solution.py:184
  66.3 0.0 copy-done
  66.3 0.9 select_reduce_fusion.1
  67.3 0.0 collective-permute-done.4
  67.3 14.6 %conditional.5 = ((f32[128,1024]{1,0:T(8,128)S(1)}, f32[128,1024]{1,0:T(8,128)S(1)})) conditional(s32[]{:T(128)} %bitcast.9, () %tuple.28, (s32[]{:T(128)}, f32[64,1024]{1,0:T(8,128)S(1)}, f32[2,1024]{1,0:T(2,128)S(1)}, f32[128,1024]{1,0:T(8,128)S(1)}) %tuple.29), branch_computations={%region_6.7_spmd, %region_7.8_spmd} | conditional | flops 131072 | bytes 4259968 | solution.py:242
  67.3 7.9 %all_to_all.52 = f32[4,16,1024]{2,1,0:T(8,128)S(1)} all-to-all(f32[4,16,1024]{2,1,0:T(8,128)S(1)} %bitcast.30), channel_id=1, replica_groups=mesh['region'=64,'zh'=2,'y'=4,'core'=2] {'y'}, dimensions={0} | all-to-all | bytes 524288 | tf_op jit(solution)/shard_map/cond/branch_1_fun/all_to_all | solution.py:181
  75.2 4.1 %collective-permute-start.1 = (f32[64,1024]{1,0:T(8,128)S(1)}, f32[64,1024]{1,0:T(8,128)S(1)}, u32[]{:S(2)}, u32[]{:S(2)}) collective-permute-start(f32[64,1024]{1,0:T(8,128)S(1)} %bitcast.28), channel_id=1, source_target_pairs={{1,0},{3,2},{5,4},{7,6},{9,8},{11,10},{13,12},{15,14},{17,16},{19,... | collective-permute-start | bytes 786440 | tf_op jit(solution)/shard_map/cond/branch_1_fun/ppermute | solution.py:178
  79.3 1.1 collective-permute-done.1
  80.5 0.7 collective-permute-start.3
  81.2 0.7 collective-permute-start.2
  81.9 0.0 collective-permute-done.3.east_ref
  81.9 0.0 collective-permute-done.2.west_ref
  81.9 47.9 %collective-permute-done.5.other_ref = f32[128,1024]{1,0:T(8,128)S(1)} collective-permute-done((f32[128,1024]{1,0:T(8,128)}, f32[128,1024]{1,0:T(8,128)S(1)}, u32[]{:S(2)}, u32[]{:S(2)}) %collective-permute-start.5) | collective-permute-done | bytes 524320 | tf_op jit(solution)/shard_map/ppermute | solution.py:175
  129.8 1.9 shard_map.56.gram_ref
  131.7 7.8 %collective-permute-start.6 = (f32[400,128]{1,0:T(8,128)S(1)}, f32[400,128]{1,0:T(8,128)S(1)}, u32[]{:S(2)}, u32[]{:S(2)}) collective-permute-start(f32[400,128]{1,0:T(8,128)S(1)} %shard_map.56.gram_ref), channel_id=1, source_target_pairs={{17,33},{33,17},{49,65},{65,49},{81,97},{97,81},{113,129},{129,113... | collective-permute-start | bytes 614408 | tf_op jit(solution)/shard_map/ppermute | solution.py:193
  139.5 1.9 collective-permute-start.9
  141.5 15.0 %collective-permute-done.6.east_ref = f32[400,128]{1,0:T(8,128)S(1)} collective-permute-done((f32[400,128]{1,0:T(8,128)S(1)}, f32[400,128]{1,0:T(8,128)S(1)}, u32[]{:S(2)}, u32[]{:S(2)}) %collective-permute-start.6) | collective-permute-done | bytes 204832 | tf_op jit(solution)/shard_map/ppermute | solution.py:193
  156.5 1.3 collective-permute-start.7
  157.8 0.0 collective-permute-done.9.west_ref
  157.8 11.8 %shard_map.58 = (f32[128,1024]{1,0:T(8,128)S(1)}, f32[128,1024]{1,0:T(8,128)S(1)}) custom-call(s32[1]{0:T(128)} %bitcast.8.on_ref, f32[400,128]{1,0:T(8,128)S(1)} %shard_map.56.gram_ref, f32[400,128]{1,0:T(8,128)S(1)} %collective-permute-done.9.west_ref, f32[400,128]{1,0:T(8,128)S(1)} %collective-permute-done.6.east_ref, ...), custom_call_target="tpu_custom_call" | custom-call | tf_op jit(solution)/shard_map/pallas_call | solution.py:225
  169.6 8.8 %collective-permute-start.10 = (f32[128,1024]{1,0:T(8,128)S(1)}, f32[128,1024]{1,0:T(8,128)S(1)}, u32[]{:S(2)}, u32[]{:S(2)}) collective-permute-start(f32[128,1024]{1,0:T(8,128)S(1)} %get-tuple-element.55), channel_id=1, source_target_pairs={{1,9},{9,1},{3,11},{11,3},{5,13},{13,5},{7,15},{15,7},{17,25},{25,... | collective-permute-start | bytes 1572872 | tf_op jit(solution)/shard_map/ppermute | solution.py:175
  178.5 0.0 collective-permute-done.7.token_ref
  178.5 0.0 copy-start.2
  178.5 0.6 copy-done.2
  179.1 0.7 collective-permute-start.8
  179.8 0.1 broadcast_select_fusion.1
  179.8 14.1 %all_to_all.53 = f32[8,16,1024]{2,1,0:T(8,128)S(1)} all-to-all(f32[8,16,1024]{2,1,0:T(8,128)S(1)} %bitcast.25), channel_id=1, replica_groups=mesh['region'=64,'zh'=2,'y'=4,'core'=2] {'y','core'}, dimensions={0} | all-to-all | bytes 1048576 | tf_op jit(solution)/shard_map/all_to_all | solution.py:184
  193.9 0.0 collective-permute-done.8
  193.9 70.0 %collective-permute-done.10 = f32[128,1024]{1,0:T(8,128)S(1)} collective-permute-done((f32[128,1024]{1,0:T(8,128)S(1)}, f32[128,1024]{1,0:T(8,128)S(1)}, u32[]{:S(2)}, u32[]{:S(2)}) %collective-permute-start.10) | collective-permute-done | bytes 524320 | tf_op jit(solution)/shard_map/ppermute | solution.py:175
  263.9 0.1 broadcast_select_fusion
  264.0 13.4 %all_to_all.54 = f32[8,16,1024]{2,1,0:T(8,128)S(1)} all-to-all(f32[8,16,1024]{2,1,0:T(8,128)S(1)} %bitcast.24), channel_id=1, replica_groups=mesh['region'=64,'zh'=2,'y'=4,'core'=2] {'y','core'}, dimensions={0} | all-to-all | bytes 1048576 | tf_op jit(solution)/shard_map/all_to_all | solution.py:184
  277.3 1.3 shard_map.59
  (9 shorter events, 0.1 us)
Async XLA Ops:
  0.0 66.3 %copy-start = (s32[16,1024]{1,0:T(8,128)S(1)}, s32[16,1024]{1,0:T(8,128)}, u32[]{:S(2)}) copy-start(s32[16,1024]{1,0:T(8,128)} %param.14) | copy-start | bytes 196612
  0.0 31.0 %copy-start.3 = (s32[16]{0:T(128)S(1)}, s32[16]{0:T(128)}, u32[]{:S(2)}) copy-start(s32[16]{0:T(128)} %param.15) | copy-start | bytes 196
  0.0 1.3 copy-start.1
  1.5 65.8 %collective-permute-start.4 = (f32[64,1024]{1,0:T(8,128)S(1)}, f32[64,1024]{1,0:T(8,128)S(1)}, u32[]{:S(2)}, u32[]{:S(2)}) collective-permute-start(f32[64,1024]{1,0:T(8,128)S(1)} %get-tuple-element.42), channel_id=1, source_target_pairs={{0,8},{8,0},{1,9},{9,1},{2,10},{10,2},{3,11},{11,3},{4,12},{12,4},... | collective-permute-start | bytes 786440 | tf_op jit(solution)/shard_map/ppermute | solution.py:172
  41.9 4.7 %collective-permute-start = (f32[64,1024]{1,0:T(8,128)S(1)}, f32[64,1024]{1,0:T(8,128)S(1)}, u32[]{:S(2)}, u32[]{:S(2)}) collective-permute-start(f32[64,1024]{1,0:T(8,128)S(1)} %bitcast.26), channel_id=1, source_target_pairs={{0,1},{2,3},{4,5},{6,7},{8,9},{10,11},{12,13},{14,15},{16,17},{18,... | collective-permute-start | bytes 786440 | tf_op jit(solution)/shard_map/cond/branch_1_fun/ppermute | solution.py:178
  47.4 82.4 %collective-permute-start.5 = (f32[128,1024]{1,0:T(8,128)}, f32[128,1024]{1,0:T(8,128)S(1)}, u32[]{:S(2)}, u32[]{:S(2)}) collective-permute-start(f32[128,1024]{1,0:T(8,128)} %get-tuple-element.69), channel_id=1, source_target_pairs={{1,9},{9,1},{3,11},{11,3},{5,13},{13,5},{7,15},{15,7},{17,25},{25,... | collective-permute-start | bytes 1572872 | tf_op jit(solution)/shard_map/ppermute | solution.py:175
  75.2 5.2 %collective-permute-start.1 = (f32[64,1024]{1,0:T(8,128)S(1)}, f32[64,1024]{1,0:T(8,128)S(1)}, u32[]{:S(2)}, u32[]{:S(2)}) collective-permute-start(f32[64,1024]{1,0:T(8,128)S(1)} %bitcast.28), channel_id=1, source_target_pairs={{1,0},{3,2},{5,4},{7,6},{9,8},{11,10},{13,12},{15,14},{17,16},{19,... | collective-permute-start | bytes 786440 | tf_op jit(solution)/shard_map/cond/branch_1_fun/ppermute | solution.py:178
  80.5 1.4 collective-permute-start.3
  81.2 0.7 collective-permute-start.2
  131.7 24.8 %collective-permute-start.6 = (f32[400,128]{1,0:T(8,128)S(1)}, f32[400,128]{1,0:T(8,128)S(1)}, u32[]{:S(2)}, u32[]{:S(2)}) collective-permute-start(f32[400,128]{1,0:T(8,128)S(1)} %shard_map.56.gram_ref), channel_id=1, source_target_pairs={{17,33},{33,17},{49,65},{65,49},{81,97},{97,81},{113,129},{129,113... | collective-permute-start | bytes 614408 | tf_op jit(solution)/shard_map/ppermute | solution.py:193
  139.5 18.3 %collective-permute-start.9 = (f32[400,128]{1,0:T(8,128)S(1)}, f32[400,128]{1,0:T(8,128)S(1)}, u32[]{:S(2)}, u32[]{:S(2)}) collective-permute-start(f32[400,128]{1,0:T(8,128)S(1)} %shard_map.56.gram_ref), channel_id=1, source_target_pairs={{1,17},{17,1},{33,49},{49,33},{65,81},{81,65},{97,113},{113,97},{1... | collective-permute-start | bytes 614408 | tf_op jit(solution)/shard_map/ppermute | solution.py:193
  156.5 21.9 %collective-permute-start.7 = (f32[8,128]{1,0:T(8,128)S(1)}, f32[8,128]{1,0:T(8,128)S(1)}, u32[]{:S(2)}, u32[]{:S(2)}) collective-permute-start(f32[8,128]{1,0:T(8,128)S(1)} %slice.8), channel_id=1, source_target_pairs={{1,0},{49,48},{65,64},{113,112},{129,128},{177,176},{193,192},{241... | collective-permute-start | bytes 12296 | tf_op jit(solution)/shard_map/ppermute | solution.py:246
  169.6 94.3 %collective-permute-start.10 = (f32[128,1024]{1,0:T(8,128)S(1)}, f32[128,1024]{1,0:T(8,128)S(1)}, u32[]{:S(2)}, u32[]{:S(2)}) collective-permute-start(f32[128,1024]{1,0:T(8,128)S(1)} %get-tuple-element.55), channel_id=1, source_target_pairs={{1,9},{9,1},{3,11},{11,3},{5,13},{13,5},{7,15},{15,7},{17,25},{25,... | collective-permute-start | bytes 1572872 | tf_op jit(solution)/shard_map/ppermute | solution.py:175
  178.5 0.6 copy-start.2
  179.1 14.9 %collective-permute-start.8 = (f32[128,1024]{1,0:T(8,128)S(1)}, f32[128,1024]{1,0:T(8,128)S(1)}, u32[]{:S(2)}, u32[]{:S(2)}) collective-permute-start(f32[128,1024]{1,0:T(8,128)S(1)} %shard_map.57), channel_id=1, source_target_pairs={{0,8},{8,0},{2,10},{10,2},{4,12},{12,4},{6,14},{14,6},{16,24},{24,... | collective-permute-start | bytes 1572872 | tf_op jit(solution)/shard_map/ppermute | solution.py:175

commit v2 on v1

--- a/solution.py
+++ b/solution.py
@@ -35,7 +35,7 @@
     return pl.pallas_call(
         lambda token_ref, x_ref, out_ref: None,
         out_shape=f32(*x.shape),
-        in_specs=[any_space] * 2,
+        in_specs=[VMEM, any_space],
         out_specs=any_space,
         input_output_aliases={1: 0},
     )(token, x)
@@ -61,14 +61,17 @@
                 own_ref[pl.ds(16 * b, 16), :] = rows(mine + b)
 
 
-def join_kernel(zh_ref, own_ref, back_ref, out_ref):
+def join_kernel(zh_ref, own_ref, first_ref, later_ref, out_ref):
     for side in range(2):
 
         @pl.when(zh_ref[0] == side)
         def _():
+            mine, theirs = 8 * side, 8 * (1 - side)
             for b in range(8):
-                out_ref[:, 8 * side + b, :] = own_ref[pl.ds(16 * b, 16), :]
-                out_ref[:, 8 * (1 - side) + b, :] = back_ref[pl.ds(16 * b, 16), :]
+                out_ref[:, mine + b, :] = own_ref[pl.ds(16 * b, 16), :]
+            for y in range(4):
+                out_ref[:, theirs + 2 * y, :] = first_ref[pl.ds(16 * y, 16), :]
+                out_ref[:, theirs + 2 * y + 1, :] = later_ref[pl.ds(16 * y, 16), :]
 
 
 def centred(own_ref, other_ref):
@@ -152,9 +155,7 @@
         average, deviation = centred(own_ref, other_ref)
         result = average + product3(weights, deviation)
         mine_ref[...] = result[:HALF]
-        for part in range(8):
-            core, y = part // 4, part % 4
-            theirs_ref[pl.ds(16 * (2 * y + core), 16), :] = result[HALF + 16 * part : HALF + 16 * part + 16]
+        theirs_ref[...] = result[HALF:]
 
 
 def shards(members, obs_value, obs_precision, obs_index, obs_count):
@@ -222,7 +223,7 @@
             on[s], table, own, other
         )
         west, east = beside(gram, s)
-        return east, call(
+        return west[:8] + east[:8], call(
             analyse_kernel,
             (f32(HALF, width), f32(HALF, width)),
             [SMEM] + [VMEM] * 5,
@@ -241,16 +242,21 @@
     crossed, own, table = lax.optimization_barrier((crossed, own, table))
     mine_0, theirs_0 = lax.cond(always, first_half, no_half, crossed, own, table)
     later_crossed, mine_0 = lax.optimization_barrier((later_crossed, mine_0))
-    east, (mine_1, theirs_1) = analysed(1, own, table, later_crossed)
-    pairs = [(2 * r + 1, 2 * r) for r in range(regions) if r % 4 in (0, 3)]
-    gone = lax.ppermute(east[:8], ("region", "core"), pairs)
-    theirs_0 = after(theirs_0, gone)
-    back_0 = swap_on(theirs_0, 0)
-    back_1 = swap_on(theirs_1, 1)
-    mine = over_y_core(jnp.where(core == 0, mine_0, mine_1))
+    neighbours, (mine_1, theirs_1) = analysed(1, own, table, later_crossed)
+    gone = to_core(neighbours, 0)
+    back_0 = swap_on(after(theirs_0, gone), 0)
+
+    def spread_back(theirs, s):
+        send, keep = jnp.split(theirs, [64]) if s else jnp.split(theirs, [64])[::-1]
+        return over_y(jnp.where(core == s, keep, to_core(send, 1 - s)))
+
+    crossing = lax.cond(always, lambda x: spread_back(x, 1), lambda x: x[:64], theirs_1)
+    back_1 = swap(crossing)
+    mine = jnp.where(core == 0, mine_0, mine_1)
+    mine = lax.cond(always, over_y_core, lambda x: x, mine)
     back_0, mine = lax.optimization_barrier((back_0, mine))
-    back = over_y_core(jnp.where(core == 0, back_0, back_1))
-    return call(join_kernel, f32(*members.shape), [SMEM] + [VMEM] * 2)(side, mine, back)
+    back_0 = lax.cond(always, lambda x: spread_back(x, 0), lambda x: x[:64], back_0)
+    return call(join_kernel, f32(*members.shape), [SMEM] + [VMEM] * 3)(side, mine, back_0, back_1)
 
 
 def solution(mesh):

time: 279 us -> 270 us (0.968)
  the two profiles are of different devices: /device:TPU:1 before, /device:TPU:6 now
where the time goes in v2:
time: 270 us; the launch traced here: 269 us
  starting transfers between devices  123 us (46%)
  blocking collectives  76.3 us (28%)
  waiting for transfers between devices  44.4 us (16%)
  Pallas kernels  15.9 us (6%)
  local copies, waits for them, and re-layouts  5.12 us (2%)
  other arithmetic  3.71 us (1%)
    ppermute x4, starting transfers between devices, beside(): found.append(lax.ppermute(x, ('region', 'core'), pairs))  58.6 us
    all_to_all x4, blocking collectives, over_y(): return lax.all_to_all(x, 'y', split_axis=0, concat_axis=0, tiled=True)  49.7 us
    ppermute x2, starting transfers between devices, swap(): return lax.ppermute(x, 'zh', [(0, 1), (1, 0)])  41.3 us
    ppermute x2, waiting for transfers between devices, swap_on(): return lax.ppermute(x, ('zh', 'core'), [(s, 2 + s), (2 + s, s)])  28.5 us
    all_to_all x2, blocking collectives, over_y_core(): lax.all_to_all(x, ('y', 'core'), split_axis=0, concat_axis=0, tiled=True)  26.6 us
    ppermute x2, starting transfers between devices, swap_on(): return lax.ppermute(x, ('zh', 'core'), [(s, 2 + s), (2 + s, s)])  16.6 us
    pallas_call x2, Pallas kernels, analysed(): call(analyse_kernel, (f32(HALF, width), f32(HALF, width)), [SMEM] + [VMEM...  11.8 us
    ppermute x5, waiting for transfers between devices, to_core(): return lax.ppermute(x, 'core', [(1 - s, s)])  8.27 us
  transfers between devices with their start and end apart: 13, of which 8 were waited for; matrix products, arithmetic and copies ran while one was open for 2% of the time, Pallas kernels for 5%

profile of v2, /device:TPU:6, one launch (start us, length us, event | category | flops | bytes accessed | tf_op | source)
XLA Modules:
  0.0 269.5 jit_solution(5812559544935324009)
XLA Ops:
  0.0 1.3 copy-done.1
  1.3 0.2 shard_map.55
  1.5 29.0 %collective-permute-start.6 = (f32[64,1024]{1,0:T(8,128)S(1)}, f32[64,1024]{1,0:T(8,128)S(1)}, u32[]{:S(2)}, u32[]{:S(2)}) collective-permute-start(f32[64,1024]{1,0:T(8,128)S(1)} %get-tuple-element.67), channel_id=1, source_target_pairs={{0,8},{8,0},{1,9},{9,1},{2,10},{10,2},{3,11},{11,3},{4,12},{12,4},... | collective-permute-start | bytes 786440 | tf_op jit(solution)/shard_map/ppermute | solution.py:173
  30.5 0.6 fusion.3
  31.8 13.4 %conditional.7 = (f32[128,1024]{1,0:T(8,128)S(1)}) conditional(s32[]{:T(128)} %bitcast.15, f32[128,1024]{1,0:T(8,128)S(1)} %get-tuple-element.68, f32[64,1024]{1,0:T(8,128)S(1)} %get-tuple-element.71), branch_computations={%region_4.5_spmd, %region_5.6_spmd} | conditional | flops 131072 | bytes 2621488 | solution.py:208
  31.8 10.9 %all_to_all.55 = f32[4,16,1024]{2,1,0:T(8,128)S(1)} all-to-all(f32[4,16,1024]{2,1,0:T(8,128)S(1)} %bitcast.34), channel_id=1, replica_groups=mesh['region'=64,'zh'=2,'y'=4,'core'=2] {'y'}, dimensions={0} | all-to-all | bytes 524288 | tf_op jit(solution)/shard_map/cond/branch_1_fun/all_to_all | solution.py:182
  42.8 1.3 collective-permute-start
  44.1 1.1 collective-permute-done
  45.2 0.7 collective-permute-start.7
  45.9 0.8 constant_dynamic-slice_fusion
  46.7 0.7 fusion.1
  47.4 13.9 %conditional.6 = (f32[128,1024]{1,0:T(8,128)S(1)}) conditional(s32[]{:T(128)} %bitcast.15, f32[128,1024]{1,0:T(8,128)S(1)} %get-tuple-element.68, f32[128,1024]{1,0:T(8,128)S(1)} %get-tuple-element.68), branch_computations={%region_0.0_spmd, %region_1.0_spmd} | conditional | bytes 2097160 | solution.py:241
  47.5 13.8 %all_to_all.54 = f32[8,16,1024]{2,1,0:T(8,128)S(1)} all-to-all(f32[8,16,1024]{2,1,0:T(8,128)S(1)} %copy.22), channel_id=1, replica_groups=mesh['region'=64,'zh'=2,'y'=4,'core'=2] {'y','core'}, dimensions={0} | all-to-all | bytes 1048576 | tf_op jit(solution)/shard_map/cond/branch_1_fun/all_to_all | solution.py:185
  61.3 0.9 select_reduce_fusion.1
  62.3 91.1 %conditional.8 = ((f32[128,1024]{1,0:T(8,128)S(1)}, f32[128,1024]{1,0:T(8,128)S(1)})) conditional(s32[]{:T(128)} %bitcast.15, () %tuple.46, (s32[]{:T(128)}, f32[64,1024]{1,0:T(8,128)S(1)}, f32[2,1024]{1,0:T(2,128)S(1)}, f32[128,1024]{1,0:T(8,128)S(1)}) %tuple.47), branch_computations={%region_6.7_spmd, %region_7.8_spmd} | conditional | flops 131072 | bytes 4259968 | solution.py:243
  62.3 9.1 %all_to_all.56 = f32[4,16,1024]{2,1,0:T(8,128)S(1)} all-to-all(f32[4,16,1024]{2,1,0:T(8,128)S(1)} %bitcast.33), channel_id=1, replica_groups=mesh['region'=64,'zh'=2,'y'=4,'core'=2] {'y'}, dimensions={0} | all-to-all | bytes 524288 | tf_op jit(solution)/shard_map/cond/branch_1_fun/all_to_all | solution.py:182
  71.4 1.3 collective-permute-start.1
  72.7 2.1 collective-permute-done.1
  74.9 1.9 branch_1_fun.2.gram_ref
  76.7 55.3 %collective-permute-start.3 = (f32[400,128]{1,0:T(8,128)S(1)}, f32[400,128]{1,0:T(8,128)S(1)}, u32[]{:S(2)}, u32[]{:S(2)}) collective-permute-start(f32[400,128]{1,0:T(8,128)S(1)} %branch_1_fun.2.gram_ref), channel_id=1, source_target_pairs={{16,32},{32,16},{48,64},{64,48},{80,96},{96,80},{112,128},{128,112... | collective-permute-start | bytes 614408 | tf_op jit(solution)/shard_map/cond/branch_1_fun/ppermute | solution.py:194
  132.1 1.9 collective-permute-start.2
  134.0 3.0 %collective-permute-done.3.east_ref = f32[400,128]{1,0:T(8,128)S(1)} collective-permute-done((f32[400,128]{1,0:T(8,128)S(1)}, f32[400,128]{1,0:T(8,128)S(1)}, u32[]{:S(2)}, u32[]{:S(2)}) %collective-permute-start.3) | collective-permute-done | bytes 204832 | tf_op jit(solution)/shard_map/cond/branch_1_fun/ppermute | solution.py:194
  137.0 4.6 %collective-permute-done.2.west_ref = f32[400,128]{1,0:T(8,128)S(1)} collective-permute-done((f32[400,128]{1,0:T(8,128)S(1)}, f32[400,128]{1,0:T(8,128)S(1)}, u32[]{:S(2)}, u32[]{:S(2)}) %collective-permute-start.2) | collective-permute-done | bytes 204832 | tf_op jit(solution)/shard_map/cond/branch_1_fun/ppermute | solution.py:194
  141.6 11.8 %branch_1_fun.3 = (f32[128,1024]{1,0:T(8,128)S(1)}, f32[128,1024]{1,0:T(8,128)S(1)}) custom-call(s32[1]{0:T(128)} %bitcast.4.on_ref, f32[400,128]{1,0:T(8,128)S(1)} %branch_1_fun.2.gram_ref, f32[400,128]{1,0:T(8,128)S(1)} %collective-permute-done.2.west_ref, f32[400,128]{1,0:T(8,128)S(1)} %collective-permute-done.3.east_ref, ...), custom_call_target="tpu_custom_call" | custom-call | tf_op jit(solution)/shard_map/cond/branch_1_fun/pallas_call | solution.py:226
  153.5 0.7 collective-permute-start.9
  154.1 0.7 collective-permute-start.8
  154.8 1.3 collective-permute-start.10
  156.1 1.8 collective-permute-done.10.token_ref
  157.9 0.6 copy-done.3
  158.5 0.7 shard_map.57
  159.2 15.9 %collective-permute-start.11 = (f32[128,1024]{1,0:T(8,128)S(1)}, f32[128,1024]{1,0:T(8,128)}, u32[]{:S(2)}, u32[]{:S(2)}) collective-permute-start(f32[128,1024]{1,0:T(8,128)S(1)} %shard_map.57), channel_id=1, source_target_pairs={{0,8},{8,0},{2,10},{10,2},{4,12},{12,4},{6,14},{14,6},{16,24},{24,... | collective-permute-start | bytes 1572872 | tf_op jit(solution)/shard_map/ppermute | solution.py:176
  175.1 14.9 %conditional.11 = (f32[64,1024]{1,0:T(8,128)S(1)}) conditional(s32[]{:T(128)} %bitcast.15, f32[128,1024]{1,0:T(8,128)S(1)} %get-tuple-element.80, (s32[]{:T(128)}, f32[128,1024]{1,0:T(8,128)S(1)}) %tuple.51), branch_computations={%region_12.13_spmd, %region_13.14_spmd} | conditional | flops 65537 | bytes 4980822 | solution.py:253
  175.2 0.8 copy-done.2
  176.0 1.3 collective-permute-start.5
  177.3 2.1 collective-permute-done.5
  179.4 1.0 slice_select_fusion.1
  180.4 9.6 %all_to_all.59 = f32[4,16,1024]{2,1,0:T(8,128)S(1)} all-to-all(f32[4,16,1024]{2,1,0:T(8,128)S(1)} %bitcast.31), channel_id=1, replica_groups=mesh['region'=64,'zh'=2,'y'=4,'core'=2] {'y'}, dimensions={0} | all-to-all | bytes 524288 | tf_op jit(solution)/shard_map/cond/branch_1_fun/all_to_all | solution.py:182
  190.0 12.3 %collective-permute-start.12 = (f32[64,1024]{1,0:T(8,128)S(1)}, f32[64,1024]{1,0:T(8,128)S(1)}, u32[]{:S(2)}, u32[]{:S(2)}) collective-permute-start(f32[64,1024]{1,0:T(8,128)S(1)} %get-tuple-element.98), channel_id=1, source_target_pairs={{0,8},{8,0},{1,9},{9,1},{2,10},{10,2},{3,11},{11,3},{4,12},{12,4},... | collective-permute-start | bytes 786440 | tf_op jit(solution)/shard_map/ppermute | solution.py:173
  202.4 12.9 %conditional.9 = (f32[128,1024]{1,0:T(8,128)S(1)}) conditional(s32[]{:T(128)} %bitcast.15, f32[128,1024]{1,0:T(8,128)S(1)} %broadcast_select_fusion, f32[128,1024]{1,0:T(8,128)S(1)} %broadcast_select_fusion), branch_computations={%region_8.9_spmd, %region_9.10_spmd} | conditional | bytes 2097160 | solution.py:256
  202.5 12.8 %all_to_all.57 = f32[8,16,1024]{2,1,0:T(8,128)S(1)} all-to-all(f32[8,16,1024]{2,1,0:T(8,128)S(1)} %copy.23), channel_id=1, replica_groups=mesh['region'=64,'zh'=2,'y'=4,'core'=2] {'y','core'}, dimensions={0} | all-to-all | bytes 1048576 | tf_op jit(solution)/shard_map/cond/branch_1_fun/all_to_all | solution.py:185
  215.3 28.5 %collective-permute-done.11 = f32[128,1024]{1,0:T(8,128)} collective-permute-done((f32[128,1024]{1,0:T(8,128)S(1)}, f32[128,1024]{1,0:T(8,128)}, u32[]{:S(2)}, u32[]{:S(2)}) %collective-permute-start.11) | collective-permute-done | bytes 524320 | tf_op jit(solution)/shard_map/ppermute | solution.py:176
  243.8 24.4 %conditional.10 = (f32[64,1024]{1,0:T(8,128)S(1)}) conditional(s32[]{:T(128)} %bitcast.15, f32[128,1024]{1,0:T(8,128)} %collective-permute-done.11, (s32[]{:T(128)}, f32[128,1024]{1,0:T(8,128)}) %tuple.50), branch_computations={%region_10.11_spmd, %region_11.12_spmd} | conditional | flops 65537 | bytes 2883642 | solution.py:258
  243.8 1.0 split.9
  244.8 1.3 collective-permute-start.4
  246.1 1.1 collective-permute-done.4
  247.2 1.0 slice_select_fusion
  248.2 20.0 %all_to_all.58 = f32[4,16,1024]{2,1,0:T(8,128)S(1)} all-to-all(f32[4,16,1024]{2,1,0:T(8,128)S(1)} %bitcast.32), channel_id=1, replica_groups=mesh['region'=64,'zh'=2,'y'=4,'core'=2] {'y'}, dimensions={0} | all-to-all | bytes 524288 | tf_op jit(solution)/shard_map/cond/branch_1_fun/all_to_all | solution.py:182
  268.2 1.2 shard_map.59
  (23 shorter events, 0.3 us)
Async XLA Ops:
  0.0 61.3 %copy-start = (s32[16,1024]{1,0:T(8,128)S(1)}, s32[16,1024]{1,0:T(8,128)}, u32[]{:S(2)}) copy-start(s32[16,1024]{1,0:T(8,128)} %param.20) | copy-start | bytes 196612
  0.0 30.5 %copy-start.4 = (s32[16]{0:T(128)S(1)}, s32[16]{0:T(128)}, u32[]{:S(2)}) copy-start(s32[16]{0:T(128)} %param.21) | copy-start | bytes 196
  0.0 1.3 copy-start.1
  1.5 60.8 %collective-permute-start.6 = (f32[64,1024]{1,0:T(8,128)S(1)}, f32[64,1024]{1,0:T(8,128)S(1)}, u32[]{:S(2)}, u32[]{:S(2)}) collective-permute-start(f32[64,1024]{1,0:T(8,128)S(1)} %get-tuple-element.67), channel_id=1, source_target_pairs={{0,8},{8,0},{1,9},{9,1},{2,10},{10,2},{3,11},{11,3},{4,12},{12,4},... | collective-permute-start | bytes 786440 | tf_op jit(solution)/shard_map/ppermute | solution.py:173
  42.8 2.4 collective-permute-start
  45.2 108.2 %collective-permute-start.7 = (f32[128,1024]{1,0:T(8,128)S(1)}, f32[128,1024]{1,0:T(8,128)S(1)}, u32[]{:S(2)}, u32[]{:S(2)}) collective-permute-start(f32[128,1024]{1,0:T(8,128)S(1)} %get-tuple-element.94), channel_id=1, source_target_pairs={{1,9},{9,1},{3,11},{11,3},{5,13},{13,5},{7,15},{15,7},{17,25},{25,... | collective-permute-start | bytes 1572872 | tf_op jit(solution)/shard_map/ppermute | solution.py:176
  71.4 3.4 %collective-permute-start.1 = (f32[64,1024]{1,0:T(8,128)S(1)}, f32[64,1024]{1,0:T(8,128)S(1)}, u32[]{:S(2)}, u32[]{:S(2)}) collective-permute-start(f32[64,1024]{1,0:T(8,128)S(1)} %bitcast.29), channel_id=1, source_target_pairs={{1,0},{3,2},{5,4},{7,6},{9,8},{11,10},{13,12},{15,14},{17,16},{19,... | collective-permute-start | bytes 786440 | tf_op jit(solution)/shard_map/cond/branch_1_fun/ppermute | solution.py:179
  76.7 60.3 %collective-permute-start.3 = (f32[400,128]{1,0:T(8,128)S(1)}, f32[400,128]{1,0:T(8,128)S(1)}, u32[]{:S(2)}, u32[]{:S(2)}) collective-permute-start(f32[400,128]{1,0:T(8,128)S(1)} %branch_1_fun.2.gram_ref), channel_id=1, source_target_pairs={{16,32},{32,16},{48,64},{64,48},{80,96},{96,80},{112,128},{128,112... | collective-permute-start | bytes 614408 | tf_op jit(solution)/shard_map/cond/branch_1_fun/ppermute | solution.py:194
  132.1 9.5 %collective-permute-start.2 = (f32[400,128]{1,0:T(8,128)S(1)}, f32[400,128]{1,0:T(8,128)S(1)}, u32[]{:S(2)}, u32[]{:S(2)}) collective-permute-start(f32[400,128]{1,0:T(8,128)S(1)} %branch_1_fun.2.gram_ref), channel_id=1, source_target_pairs={{0,16},{16,0},{32,48},{48,32},{64,80},{80,64},{96,112},{112,96},{1... | collective-permute-start | bytes 614408 | tf_op jit(solution)/shard_map/cond/branch_1_fun/ppermute | solution.py:194
  153.5 1.4 collective-permute-start.9
  154.1 0.7 collective-permute-start.8
  154.8 3.1 %collective-permute-start.10 = (f32[8,128]{1,0:T(8,128)S(1)}, f32[8,128]{1,0:T(8,128)S(1)}, u32[]{:S(2)}, u32[]{:S(2)}) collective-permute-start(f32[8,128]{1,0:T(8,128)S(1)} %slice_add_fusion), channel_id=1, source_target_pairs={{1,0},{3,2},{5,4},{7,6},{9,8},{11,10},{13,12},{15,14},{17,16},{19,... | collective-permute-start | bytes 12296 | tf_op jit(solution)/shard_map/ppermute | solution.py:179
  157.9 0.6 copy-start.3
  159.2 84.6 %collective-permute-start.11 = (f32[128,1024]{1,0:T(8,128)S(1)}, f32[128,1024]{1,0:T(8,128)}, u32[]{:S(2)}, u32[]{:S(2)}) collective-permute-start(f32[128,1024]{1,0:T(8,128)S(1)} %shard_map.57), channel_id=1, source_target_pairs={{0,8},{8,0},{2,10},{10,2},{4,12},{12,4},{6,14},{14,6},{16,24},{24,... | collective-permute-start | bytes 1572872 | tf_op jit(solution)/shard_map/ppermute | solution.py:176
  175.2 0.8 copy-start.2
  176.0 3.4 %collective-permute-start.5 = (f32[64,1024]{1,0:T(8,128)S(1)}, f32[64,1024]{1,0:T(8,128)S(1)}, u32[]{:S(2)}, u32[]{:S(2)}) collective-permute-start(f32[64,1024]{1,0:T(8,128)S(1)} %split.11), channel_id=1, source_target_pairs={{1,0},{3,2},{5,4},{7,6},{9,8},{11,10},{13,12},{15,14},{17,16},{19,... | collective-permute-start | bytes 786440 | tf_op jit(solution)/shard_map/cond/branch_1_fun/ppermute | solution.py:179
  190.0 78.2 %collective-permute-start.12 = (f32[64,1024]{1,0:T(8,128)S(1)}, f32[64,1024]{1,0:T(8,128)S(1)}, u32[]{:S(2)}, u32[]{:S(2)}) collective-permute-start(f32[64,1024]{1,0:T(8,128)S(1)} %get-tuple-element.98), channel_id=1, source_target_pairs={{0,8},{8,0},{1,9},{9,1},{2,10},{10,2},{3,11},{11,3},{4,12},{12,4},... | collective-permute-start | bytes 786440 | tf_op jit(solution)/shard_map/ppermute | solution.py:173
  244.8 2.4 collective-permute-start.4

commit v3 on v2

v3 whole, which is shorter than its diff:
```python
import functools
import math

import jax
import jax.numpy as jnp
from jax import lax
from jax.experimental import pallas as pl
from jax.experimental.pallas import tpu as pltpu
from jax.sharding import Mesh
from jax.sharding import PartitionSpec as P

K = 256
ITERS = 12
HALF = K // 2
MEMBER = ("zh", "y", "core")
HIGHEST = lax.Precision.HIGHEST
VMEM = pl.BlockSpec(memory_space=pltpu.VMEM)
SMEM = pl.BlockSpec(memory_space=pltpu.SMEM)


def call(kernel, outs, specs, scratch=()):
    return pl.pallas_call(
        kernel,
        out_shape=outs,
        in_specs=specs,
        out_specs=jax.tree.map(lambda _: VMEM, outs),
        scratch_shapes=list(scratch),
        compiler_params=pltpu.CompilerParams(vmem_limit_bytes=24 << 20),
        cost_estimate=pl.CostEstimate(flops=0, bytes_accessed=0, transcendentals=0),
    )


def f32(*shape):
    return jax.ShapeDtypeStruct(shape, jnp.float32)


def split_kernel(zh_ref, x_ref, first_ref, own_ref, later_ref):
    def rows(band):
        return x_ref[:, band, :]

    for side in range(2):

        @pl.when(zh_ref[0] == side)
        def _():
            mine, theirs = 8 * side, 8 * (1 - side)
            for y in range(4):
                first_ref[pl.ds(16 * y, 16), :] = rows(theirs + 2 * y)
                later_ref[pl.ds(16 * y, 16), :] = rows(theirs + 2 * y + 1)
            for b in range(8):
                own_ref[pl.ds(16 * b, 16), :] = rows(mine + b)


def join_kernel(zh_ref, own_ref, first_ref, later_ref, out_ref):
    for side in range(2):

        @pl.when(zh_ref[0] == side)
        def _():
            mine, theirs = 8 * side, 8 * (1 - side)
            for b in range(8):
                out_ref[:, mine + b, :] = own_ref[pl.ds(16 * b, 16), :]
            for y in range(4):
                out_ref[:, theirs + 2 * y, :] = first_ref[pl.ds(16 * y, 16), :]
                out_ref[:, theirs + 2 * y + 1, :] = later_ref[pl.ds(16 * y, 16), :]


def product(a, b):
    return jnp.dot(a, b, precision=HIGHEST, preferred_element_type=jnp.float32)


def across(a, b):
    return lax.dot_general(
        a, b, (((1,), (1,)), ((), ())), precision=HIGHEST, preferred_element_type=jnp.float32
    )


def gram_kernel(core_ref, table_ref, own_ref, early_ref, late_ref, gram_ref, average_ref, deviation_ref):
    other = jnp.where(core_ref[0] == 0, early_ref[...], late_ref[...])
    states = jnp.concatenate([own_ref[...], other], axis=0)
    average = jnp.sum(states, axis=0, keepdims=True) / K
    deviation = states - average
    average_ref[...] = jnp.broadcast_to(average, average_ref.shape)
    deviation_ref[...] = deviation
    weight, pull = table_ref[0:1, :], table_ref[1:2, :]
    scaled = deviation * jnp.sqrt(weight)
    gram = across(scaled, scaled)
    right = across(jnp.broadcast_to(pull - weight * average, average_ref.shape), deviation)
    gram_ref[0:128, :] = gram[:HALF, :HALF]
    gram_ref[128:256, :] = gram[:HALF, HALF:]
    gram_ref[256:384, :] = gram[HALF:, HALF:]
    gram_ref[384:392, :] = right[:, :HALF]
    gram_ref[392:400, :] = right[:, HALF:]


def two_parts(x):
    high = x.astype(jnp.bfloat16)
    return high, (x - high.astype(jnp.float32)).astype(jnp.bfloat16)


def product3(a, b):
    (ah, al), (bh, bl) = two_parts(a), two_parts(b)
    dot = functools.partial(jnp.dot, preferred_element_type=jnp.float32)
    return dot(ah, bh) + (dot(ah, bl) + dot(al, bh))


def analyse_kernel(
    core_ref, gram_ref, west_ref, east_ref, average_ref, deviation_ref, mine_ref, keep_ref, send_ref, u_ref, z_ref
):
    total = gram_ref[...] + 0.5 * (west_ref[...] + east_ref[...])
    g11, g12, g22 = total[:128], total[128:256], total[256:384]
    right = jnp.concatenate([total[384:385], total[392:393]], axis=1)
    gram = jnp.concatenate(
        [jnp.concatenate([g11, g12], axis=1), jnp.concatenate([g12.T, g22], axis=1)], axis=0
    )
    rows = lax.broadcasted_iota(jnp.int32, (K, K), 0)
    columns = lax.broadcasted_iota(jnp.int32, (K, K), 1)
    diagonal = rows == columns
    system = gram + jnp.where(diagonal, K - 1.0, 0.0)
    factor = jnp.sqrt(jnp.sum(system * system, keepdims=True) + 1e-06)
    three = jnp.where(diagonal, 3.0, 0.0)
    root = system / factor
    middle = three - root
    u_ref[...] = 0.5 * product(root, middle)
    z_ref[...] = 0.5 * middle

    def sweep(_, carry):
        root, inverse = u_ref[...], z_ref[...]
        middle = three - product(inverse, root)
        u_ref[...] = 0.5 * product(root, middle)
        z_ref[...] = 0.5 * product(middle, inverse)
        return carry

    lax.fori_loop(0, ITERS - 2, sweep, 0)
    root, inverse = u_ref[...], z_ref[...]
    inverse = 0.5 * product(three - product(inverse, root), inverse)
    inverse = inverse / jnp.sqrt(factor)
    pulled = jnp.sum(inverse * right, axis=1, keepdims=True)
    shift = jnp.sum(inverse * pulled, axis=0, keepdims=True)
    weights = math.sqrt(K - 1.0) * inverse + shift
    result = average_ref[0:1, :] + product3(weights, deviation_ref[...])
    mine_ref[...] = result[:HALF]
    quarter = HALF // 2
    for core in range(2):

        @pl.when(core_ref[0] == core)
        def _():
            keep_ref[...] = result[HALF + core * quarter :][:quarter]
            send_ref[...] = result[HALF + (1 - core) * quarter :][:quarter]


def shards(members, obs_value, obs_precision, obs_index, obs_count):
    zh, y, core = (lax.axis_index(a) for a in MEMBER)
    regions = lax.axis_size("region")
    width = members.shape[2]
    side = zh.astype(jnp.int32).reshape(1)
    which = core.astype(jnp.int32).reshape(1)

    first, own, later = call(
        split_kernel, (f32(64, width), f32(128, width), f32(64, width)), [SMEM, VMEM]
    )(side, members)

    def swap(x):
        return lax.ppermute(x, "zh", [(0, 1), (1, 0)])

    def swap_on(x, s):
        return lax.ppermute(x, ("zh", "core"), [(s, 2 + s), (2 + s, s)])

    def to_core(x, s):
        return lax.ppermute(x, "core", [(1 - s, s)])

    def over_y(x):
        return lax.all_to_all(x, "y", split_axis=0, concat_axis=0, tiled=True)

    def over_y_core(x):
        return lax.all_to_all(x, ("y", "core"), split_axis=0, concat_axis=0, tiled=True)

    def beside(x):
        found = []
        for odd in (0, 1):
            ahead = [(r, (r + 1) % regions) for r in range(odd, regions, 2)]
            found.append(lax.ppermute(x, "region", ahead + [(b, a) for a, b in ahead]))
        return found

    crossed = swap(first)
    always = obs_count[0] > 0

    def spread(later, own):
        near = over_y(later)
        far = to_core(near, 1)
        return jnp.concatenate([far, near]).reshape(HALF, width)

    def no_spread(later, own):
        return own.reshape(HALF, width)

    later = lax.cond(always, spread, no_spread, later, own)
    later_crossed = swap_on(later, 1)

    band = zh * 8 + y * 2 + core
    pick = lambda t: lax.dynamic_index_in_dim(t, band, 0, keepdims=False)
    places, observed, accuracy, filled = map(pick, (obs_index, obs_value, obs_precision, obs_count))
    slots = jnp.arange(width, dtype=jnp.int32)
    accuracy = jnp.where(slots < filled, accuracy, 0.0)
    hit = places[:, None] == slots[None, :]
    weight = jnp.sum(jnp.where(hit, accuracy[:, None], 0.0), axis=0)
    pull = jnp.sum(jnp.where(hit, (accuracy * observed)[:, None], 0.0), axis=0)
    table = jnp.stack([weight, pull])

    def gathered(crossed):
        near = over_y(crossed)
        far = to_core(near, 0)
        return jnp.concatenate([near, far]).reshape(HALF, width)

    own = lax.cond(always, over_y_core, lambda x: x, own)
    crossed, own, table = lax.optimization_barrier((crossed, own, table))
    early = lax.cond(always, gathered, lambda x: jnp.concatenate([x, x]).reshape(HALF, width), crossed)
    later_crossed, early = lax.optimization_barrier((later_crossed, early))

    gram, average, deviation = call(
        gram_kernel, (f32(400, 128), f32(8, width), f32(K, width)), [SMEM] + [VMEM] * 4
    )(which, table, own, early, later_crossed)
    west, east = beside(gram)
    mine, keep, send = call(
        analyse_kernel,
        (f32(HALF, width), f32(64, width), f32(64, width)),
        [SMEM] + [VMEM] * 5,
        scratch=[pltpu.VMEM((K, K), jnp.float32)] * 2,
    )(which, gram, west, east, average, deviation)

    got = lax.ppermute(send, "core", [(0, 1), (1, 0)])
    back_0 = swap(jnp.where(core == 0, keep, got))
    crossing = lax.cond(always, over_y, lambda x: x, jnp.where(core == 0, got, keep))
    back_1 = swap(crossing)
    crossing, mine = lax.optimization_barrier((crossing, mine))
    mine = lax.cond(always, over_y_core, lambda x: x, mine)
    back_0, mine = lax.optimization_barrier((back_0, mine))
    back_0 = lax.cond(always, over_y, lambda x: x, back_0)
    return call(join_kernel, f32(*members.shape), [SMEM] + [VMEM] * 3)(side, mine, back_0, back_1)


def solution(mesh):
    split = Mesh(
        mesh.devices.reshape(mesh.shape["region"], 2, 4, 2), ("region", "zh", "y", "core")
    )
    placed = (
        P(MEMBER, "region", None),
        P("region", None),
        P("region", None),
        P("region", None),
        P("region"),
    )
    return jax.shard_map(
        shards, mesh=split, in_specs=placed, out_specs=P(MEMBER, "region", None), check_vma=False
    )
```

time: 270 us -> 269 us (level)
  the two profiles are of different devices: /device:TPU:6 before, /device:TPU:64 now
where the time goes in v3:
time: 269 us; the launch traced here: 268 us
  starting transfers between devices  115 us (43%)
  blocking collectives  83.3 us (31%)
  waiting for transfers between devices  49.1 us (18%)
  Pallas kernels  15.2 us (6%)
  local copies, waits for them, and re-layouts  2.79 us (1%)
    all_to_all x4, blocking collectives, over_y(): return lax.all_to_all(x, 'y', split_axis=0, concat_axis=0, tiled=True)  56.7 us
    ppermute x2, starting transfers between devices, beside(): found.append(lax.ppermute(x, 'region', ahead + [(b, a) for a, b in ahead]))  54.1 us
    ppermute x3, starting transfers between devices, swap(): return lax.ppermute(x, 'zh', [(0, 1), (1, 0)])  53.5 us
    ppermute x3, waiting for transfers between devices, swap(): return lax.ppermute(x, 'zh', [(0, 1), (1, 0)])  39.4 us
    all_to_all x2, blocking collectives, over_y_core(): lax.all_to_all(x, ('y', 'core'), split_axis=0, concat_axis=0, tiled=True)  26.6 us
    pallas_call x1, Pallas kernels, shards(): call(analyse_kernel, (f32(HALF, width), f32(64, width), f32(64, width)),...  11.8 us
    ppermute x2, waiting for transfers between devices, beside(): found.append(lax.ppermute(x, 'region', ahead + [(b, a) for a, b in ahead]))  5.4 us
  transfers between devices with their start and end apart: 9, of which 5 were waited for; matrix products, arithmetic and copies ran while one was open for 1% of the time, Pallas kernels for 0%

profile of v3, /device:TPU:64, one launch (start us, length us, event | category | flops | bytes accessed | tf_op | source)
XLA Modules:
  0.0 268.0 jit_solution(2516563986429869265)
XLA Ops:
  0.0 0.0 copy-start
  0.0 0.0 copy-start.2
  0.0 0.0 copy-start.1
  0.0 1.3 copy-done.1
  1.3 0.2 shard_map.55
  1.5 27.2 %collective-permute-start.2 = (f32[64,1024]{1,0:T(8,128)S(1)}, f32[64,1024]{1,0:T(8,128)S(1)}, u32[]{:S(2)}, u32[]{:S(2)}) collective-permute-start(f32[64,1024]{1,0:T(8,128)S(1)} %get-tuple-element.52), channel_id=1, source_target_pairs={{0,8},{8,0},{1,9},{9,1},{2,10},{10,2},{3,11},{11,3},{4,12},{12,4},... | collective-permute-start | bytes 786440 | tf_op jit(solution)/shard_map/ppermute | solution.py:162
  28.7 0.0 copy-done.2
  28.7 0.6 fusion.3
  30.0 13.4 %conditional.7 = (f32[128,1024]{1,0:T(8,128)S(1)}) conditional(s32[]{:T(128)} %bitcast.14, f32[128,1024]{1,0:T(8,128)S(1)} %get-tuple-element.53, f32[64,1024]{1,0:T(8,128)S(1)} %get-tuple-element.56), branch_computations={%region_4.5_spmd, %region_5.6_spmd} | conditional | flops 131072 | bytes 2621488 | solution.py:194
  30.0 10.9 %all_to_all.55 = f32[4,16,1024]{2,1,0:T(8,128)S(1)} all-to-all(f32[4,16,1024]{2,1,0:T(8,128)S(1)} %bitcast.34), channel_id=1, replica_groups=mesh['region'=64,'zh'=2,'y'=4,'core'=2] {'y'}, dimensions={0} | all-to-all | bytes 524288 | tf_op jit(solution)/shard_map/cond/branch_1_fun/all_to_all | solution.py:171
  40.9 1.3 collective-permute-start
  42.2 1.1 collective-permute-done
  43.4 0.7 collective-permute-start.3
  44.1 0.8 constant_dynamic-slice_fusion
  44.9 0.6 fusion.1
  45.5 13.9 %conditional.6 = (f32[128,1024]{1,0:T(8,128)S(1)}) conditional(s32[]{:T(128)} %bitcast.14, f32[128,1024]{1,0:T(8,128)S(1)} %get-tuple-element.53, f32[128,1024]{1,0:T(8,128)S(1)} %get-tuple-element.53), branch_computations={%region_0.0_spmd, %region_1.0_spmd} | conditional | bytes 2097160 | solution.py:212
  45.6 13.8 %all_to_all.54 = f32[8,16,1024]{2,1,0:T(8,128)S(1)} all-to-all(f32[8,16,1024]{2,1,0:T(8,128)S(1)} %copy.18), channel_id=1, replica_groups=mesh['region'=64,'zh'=2,'y'=4,'core'=2] {'y','core'}, dimensions={0} | all-to-all | bytes 1048576 | tf_op jit(solution)/shard_map/cond/branch_1_fun/all_to_all | solution.py:174
  59.4 0.0 copy-done
  59.4 0.9 select_reduce_fusion.1
  60.4 0.0 collective-permute-done.2
  60.4 19.5 %conditional.8 = (f32[128,1024]{1,0:T(8,128)S(1)}) conditional(s32[]{:T(128)} %bitcast.14, f32[64,1024]{1,0:T(8,128)S(1)} %collective-permute-done.2, f32[64,1024]{1,0:T(8,128)S(1)} %collective-permute-done.2), branch_computations={%region_6.7_spmd, %region_7.8_spmd} | conditional | flops 131072 | bytes 2621488 | solution.py:214
  60.4 16.0 %all_to_all.56 = f32[4,16,1024]{2,1,0:T(8,128)S(1)} all-to-all(f32[4,16,1024]{2,1,0:T(8,128)S(1)} %bitcast.25), channel_id=1, replica_groups=mesh['region'=64,'zh'=2,'y'=4,'core'=2] {'y'}, dimensions={0} | all-to-all | bytes 524288 | tf_op jit(solution)/shard_map/cond/branch_1_fun/all_to_all | solution.py:171
  76.5 1.3 collective-permute-start.1
  77.8 2.1 collective-permute-done.1
  80.0 0.0 collective-permute-done.3.late_ref
  80.0 2.0 shard_map.56
  81.9 1.9 collective-permute-start.4
  83.9 52.2 %collective-permute-start.5 = (f32[400,128]{1,0:T(8,128)S(1)}, f32[400,128]{1,0:T(8,128)S(1)}, u32[]{:S(2)}, u32[]{:S(2)}) collective-permute-start(f32[400,128]{1,0:T(8,128)S(1)} %get-tuple-element.60.gram_ref), channel_id=1, source_target_pairs={{16,32},{48,64},{80,96},{112,128},{144,160},{176,192},{208,224},{2... | collective-permute-start | bytes 614408 | tf_op jit(solution)/shard_map/ppermute | solution.py:180
  136.1 0.0 collective-permute-done.4.west_ref
  136.1 5.4 %collective-permute-done.5.east_ref = f32[400,128]{1,0:T(8,128)S(1)} collective-permute-done((f32[400,128]{1,0:T(8,128)S(1)}, f32[400,128]{1,0:T(8,128)S(1)}, u32[]{:S(2)}, u32[]{:S(2)}) %collective-permute-start.5) | collective-permute-done | bytes 204832 | tf_op jit(solution)/shard_map/ppermute | solution.py:180
  141.5 11.8 %shard_map.57 = (f32[128,1024]{1,0:T(8,128)S(1)}, f32[64,1024]{1,0:T(8,128)S(1)}, f32[64,1024]{1,0:T(8,128)S(1)}) custom-call(s32[1]{0:T(128)} %bitcast.13.core_ref, f32[400,128]{1,0:T(8,128)S(1)} %get-tuple-element.60.gram_ref, f32[400,128]{1,0:T(8,128)S(1)} %collective-permute-done.4.west_ref, f32[400,128]{1,0:T(8,128)S(1)} %collective-permute-done.5.east_ref, ...), custom_call_target="tpu_custom_call" | custom-call | tf_op jit(solution)/shard_map/pallas_call | solution.py:221
  153.3 3.9 %collective-permute-start.6 = (f32[64,1024]{1,0:T(8,128)S(1)}, f32[64,1024]{1,0:T(8,128)S(1)}, u32[]{:S(2)}, u32[]{:S(2)}) collective-permute-start(f32[64,1024]{1,0:T(8,128)S(1)} %get-tuple-element.64), channel_id=1, source_target_pairs={{0,1},{1,0},{2,3},{3,2},{4,5},{5,4},{6,7},{7,6},{8,9},{9,8},{10,11... | collective-permute-start | bytes 786440 | tf_op jit(solution)/shard_map/ppermute | solution.py:228
  157.2 1.1 collective-permute-done.6
  158.4 20.0 %collective-permute-start.7 = (f32[64,1024]{1,0:T(8,128)S(1)}, f32[64,1024]{1,0:T(8,128)S(1)}, u32[]{:S(2)}, u32[]{:S(2)}) collective-permute-start(f32[64,1024]{1,0:T(8,128)S(1)} %get-tuple-element.74), channel_id=1, source_target_pairs={{0,8},{8,0},{1,9},{9,1},{2,10},{10,2},{3,11},{11,3},{4,12},{12,4},... | collective-permute-start | bytes 786440 | tf_op jit(solution)/shard_map/ppermute | solution.py:162
  178.4 9.4 %conditional.9 = (f32[64,1024]{1,0:T(8,128)S(1)}) conditional(s32[]{:T(128)} %bitcast.14, f32[64,1024]{1,0:T(8,128)S(1)} %get-tuple-element.73, f32[64,1024]{1,0:T(8,128)S(1)} %get-tuple-element.73), branch_computations={%region_8.9_spmd, %region_9.10_spmd} | conditional | bytes 1048584 | solution.py:230
  178.4 9.4 %all_to_all.57 = f32[4,16,1024]{2,1,0:T(8,128)S(1)} all-to-all(f32[4,16,1024]{2,1,0:T(8,128)S(1)} %copy.19), channel_id=1, replica_groups=mesh['region'=64,'zh'=2,'y'=4,'core'=2] {'y'}, dimensions={0} | all-to-all | bytes 524288 | tf_op jit(solution)/shard_map/cond/branch_1_fun/all_to_all | solution.py:171
  187.8 6.4 %collective-permute-start.8 = (f32[64,1024]{1,0:T(8,128)S(1)}, f32[64,1024]{1,0:T(8,128)S(1)}, u32[]{:S(2)}, u32[]{:S(2)}) collective-permute-start(f32[64,1024]{1,0:T(8,128)S(1)} %get-tuple-element.82), channel_id=1, source_target_pairs={{0,8},{8,0},{1,9},{9,1},{2,10},{10,2},{3,11},{11,3},{4,12},{12,4},... | collective-permute-start | bytes 786440 | tf_op jit(solution)/shard_map/ppermute | solution.py:162
  194.2 12.9 %conditional.10 = (f32[128,1024]{1,0:T(8,128)S(1)}) conditional(s32[]{:T(128)} %bitcast.14, f32[128,1024]{1,0:T(8,128)S(1)} %get-tuple-element.66, f32[128,1024]{1,0:T(8,128)S(1)} %get-tuple-element.66), branch_computations={%region_10.11_spmd, %region_11.12_spmd} | conditional | bytes 2097160 | solution.py:233
  194.2 12.8 %all_to_all.58 = f32[8,16,1024]{2,1,0:T(8,128)S(1)} all-to-all(f32[8,16,1024]{2,1,0:T(8,128)S(1)} %copy.20), channel_id=1, replica_groups=mesh['region'=64,'zh'=2,'y'=4,'core'=2] {'y','core'}, dimensions={0} | all-to-all | bytes 1048576 | tf_op jit(solution)/shard_map/cond/branch_1_fun/all_to_all | solution.py:174
  207.0 39.3 %collective-permute-done.7 = f32[64,1024]{1,0:T(8,128)S(1)} collective-permute-done((f32[64,1024]{1,0:T(8,128)S(1)}, f32[64,1024]{1,0:T(8,128)S(1)}, u32[]{:S(2)}, u32[]{:S(2)}) %collective-permute-start.7) | collective-permute-done | bytes 262176 | tf_op jit(solution)/shard_map/ppermute | solution.py:162
  246.4 20.4 %conditional.11 = (f32[64,1024]{1,0:T(8,128)S(1)}) conditional(s32[]{:T(128)} %bitcast.14, f32[64,1024]{1,0:T(8,128)S(1)} %collective-permute-done.7, f32[64,1024]{1,0:T(8,128)S(1)} %collective-permute-done.7), branch_computations={%region_12.13_spmd, %region_13.14_spmd} | conditional | bytes 1048584 | solution.py:235
  246.4 20.3 %all_to_all.59 = f32[4,16,1024]{2,1,0:T(8,128)S(1)} all-to-all(f32[4,16,1024]{2,1,0:T(8,128)S(1)} %copy.21), channel_id=1, replica_groups=mesh['region'=64,'zh'=2,'y'=4,'core'=2] {'y'}, dimensions={0} | all-to-all | bytes 524288 | tf_op jit(solution)/shard_map/cond/branch_1_fun/all_to_all | solution.py:171
  266.7 0.0 collective-permute-done.8.later_ref
  266.7 1.2 shard_map.58
  (9 shorter events, 0.3 us)
Async XLA Ops:
  0.0 59.4 %copy-start = (s32[16,1024]{1,0:T(8,128)S(1)}, s32[16,1024]{1,0:T(8,128)}, u32[]{:S(2)}) copy-start(s32[16,1024]{1,0:T(8,128)} %param.20) | copy-start | bytes 196612
  0.0 28.7 %copy-start.2 = (s32[16]{0:T(128)S(1)}, s32[16]{0:T(128)}, u32[]{:S(2)}) copy-start(s32[16]{0:T(128)} %param.21) | copy-start | bytes 196
  0.0 1.3 copy-start.1
  1.5 58.9 %collective-permute-start.2 = (f32[64,1024]{1,0:T(8,128)S(1)}, f32[64,1024]{1,0:T(8,128)S(1)}, u32[]{:S(2)}, u32[]{:S(2)}) collective-permute-start(f32[64,1024]{1,0:T(8,128)S(1)} %get-tuple-element.52), channel_id=1, source_target_pairs={{0,8},{8,0},{1,9},{9,1},{2,10},{10,2},{3,11},{11,3},{4,12},{12,4},... | collective-permute-start | bytes 786440 | tf_op jit(solution)/shard_map/ppermute | solution.py:162
  40.9 2.4 collective-permute-start
  43.4 36.6 %collective-permute-start.3 = (f32[128,1024]{1,0:T(8,128)S(1)}, f32[128,1024]{1,0:T(8,128)S(1)}, u32[]{:S(2)}, u32[]{:S(2)}) collective-permute-start(f32[128,1024]{1,0:T(8,128)S(1)} %get-tuple-element.80), channel_id=1, source_target_pairs={{1,9},{9,1},{3,11},{11,3},{5,13},{13,5},{7,15},{15,7},{17,25},{25,... | collective-permute-start | bytes 1572872 | tf_op jit(solution)/shard_map/ppermute | solution.py:165
  76.5 3.4 %collective-permute-start.1 = (f32[64,1024]{1,0:T(8,128)S(1)}, f32[64,1024]{1,0:T(8,128)S(1)}, u32[]{:S(2)}, u32[]{:S(2)}) collective-permute-start(f32[64,1024]{1,0:T(8,128)S(1)} %bitcast.32), channel_id=1, source_target_pairs={{1,0},{3,2},{5,4},{7,6},{9,8},{11,10},{13,12},{15,14},{17,16},{19,... | collective-permute-start | bytes 786440 | tf_op jit(solution)/shard_map/cond/branch_1_fun/ppermute | solution.py:168
  81.9 54.1 %collective-permute-start.4 = (f32[400,128]{1,0:T(8,128)S(1)}, f32[400,128]{1,0:T(8,128)S(1)}, u32[]{:S(2)}, u32[]{:S(2)}) collective-permute-start(f32[400,128]{1,0:T(8,128)S(1)} %get-tuple-element.60.gram_ref), channel_id=1, source_target_pairs={{0,16},{32,48},{64,80},{96,112},{128,144},{160,176},{192,208},{224... | collective-permute-start | bytes 614408 | tf_op jit(solution)/shard_map/ppermute | solution.py:180
  83.9 57.6 %collective-permute-start.5 = (f32[400,128]{1,0:T(8,128)S(1)}, f32[400,128]{1,0:T(8,128)S(1)}, u32[]{:S(2)}, u32[]{:S(2)}) collective-permute-start(f32[400,128]{1,0:T(8,128)S(1)} %get-tuple-element.60.gram_ref), channel_id=1, source_target_pairs={{16,32},{48,64},{80,96},{112,128},{144,160},{176,192},{208,224},{2... | collective-permute-start | bytes 614408 | tf_op jit(solution)/shard_map/ppermute | solution.py:180
  153.3 5.1 %collective-permute-start.6 = (f32[64,1024]{1,0:T(8,128)S(1)}, f32[64,1024]{1,0:T(8,128)S(1)}, u32[]{:S(2)}, u32[]{:S(2)}) collective-permute-start(f32[64,1024]{1,0:T(8,128)S(1)} %get-tuple-element.64), channel_id=1, source_target_pairs={{0,1},{1,0},{2,3},{3,2},{4,5},{5,4},{6,7},{7,6},{8,9},{9,8},{10,11... | collective-permute-start | bytes 786440 | tf_op jit(solution)/shard_map/ppermute | solution.py:228
  158.4 88.0 %collective-permute-start.7 = (f32[64,1024]{1,0:T(8,128)S(1)}, f32[64,1024]{1,0:T(8,128)S(1)}, u32[]{:S(2)}, u32[]{:S(2)}) collective-permute-start(f32[64,1024]{1,0:T(8,128)S(1)} %get-tuple-element.74), channel_id=1, source_target_pairs={{0,8},{8,0},{1,9},{9,1},{2,10},{10,2},{3,11},{11,3},{4,12},{12,4},... | collective-permute-start | bytes 786440 | tf_op jit(solution)/shard_map/ppermute | solution.py:162
  187.8 79.0 %collective-permute-start.8 = (f32[64,1024]{1,0:T(8,128)S(1)}, f32[64,1024]{1,0:T(8,128)S(1)}, u32[]{:S(2)}, u32[]{:S(2)}) collective-permute-start(f32[64,1024]{1,0:T(8,128)S(1)} %get-tuple-element.82), channel_id=1, source_target_pairs={{0,8},{8,0},{1,9},{9,1},{2,10},{10,2},{3,11},{11,3},{4,12},{12,4},... | collective-permute-start | bytes 786440 | tf_op jit(solution)/shard_map/ppermute | solution.py:162

commit v4 on v3

--- a/solution.py
+++ b/solution.py
@@ -50,7 +50,7 @@
                 own_ref[pl.ds(16 * b, 16), :] = rows(mine + b)
 
 
-def join_kernel(zh_ref, own_ref, first_ref, later_ref, out_ref):
+def join_kernel(zh_ref, own_ref, a_ref, b_ref, c_ref, d_ref, out_ref):
     for side in range(2):
 
         @pl.when(zh_ref[0] == side)
@@ -59,8 +59,10 @@
             for b in range(8):
                 out_ref[:, mine + b, :] = own_ref[pl.ds(16 * b, 16), :]
             for y in range(4):
-                out_ref[:, theirs + 2 * y, :] = first_ref[pl.ds(16 * y, 16), :]
-                out_ref[:, theirs + 2 * y + 1, :] = later_ref[pl.ds(16 * y, 16), :]
+                out_ref[0:8, theirs + 2 * y, :] = a_ref[y]
+                out_ref[8:16, theirs + 2 * y, :] = b_ref[y]
+                out_ref[0:8, theirs + 2 * y + 1, :] = c_ref[y]
+                out_ref[8:16, theirs + 2 * y + 1, :] = d_ref[y]
 
 
 def product(a, b):
@@ -226,14 +228,22 @@
     )(which, gram, west, east, average, deviation)
 
     got = lax.ppermute(send, "core", [(0, 1), (1, 0)])
-    back_0 = swap(jnp.where(core == 0, keep, got))
-    crossing = lax.cond(always, over_y, lambda x: x, jnp.where(core == 0, got, keep))
-    back_1 = swap(crossing)
+    lower = jnp.where(core == 0, keep, got).reshape(4, 16, width)
+    upper = jnp.where(core == 0, got, keep).reshape(4, 16, width)
+    back_0 = swap(lower[:, :8])
+    crossing = lax.cond(
+        always,
+        lambda x, y: over_y(jnp.concatenate([x, y], axis=1)),
+        lambda x, y: jnp.concatenate([y, x], axis=1),
+        lower[:, 8:],
+        upper,
+    )
+    rest = [swap(crossing[:, 8 * k : 8 * k + 8]) for k in range(3)]
     crossing, mine = lax.optimization_barrier((crossing, mine))
     mine = lax.cond(always, over_y_core, lambda x: x, mine)
     back_0, mine = lax.optimization_barrier((back_0, mine))
     back_0 = lax.cond(always, over_y, lambda x: x, back_0)
-    return call(join_kernel, f32(*members.shape), [SMEM] + [VMEM] * 3)(side, mine, back_0, back_1)
+    return call(join_kernel, f32(*members.shape), [SMEM] + [VMEM] * 5)(side, mine, back_0, *rest)
 
 
 def solution(mesh):

time: 269 us -> 277 us (1.030)
  the two profiles are of different devices: /device:TPU:64 before, /device:TPU:1 now
where the time goes in v4:
time: 277 us; the launch traced here: 274 us
  starting transfers between devices  99.2 us (36%)
  waiting for transfers between devices  91.8 us (33%)
  blocking collectives  61.7 us (22%)
  Pallas kernels  15.2 us (5%)
  local copies, waits for them, and re-layouts  2.86 us (1%)
    ppermute x5, starting transfers between devices, swap(): return lax.ppermute(x, 'zh', [(0, 1), (1, 0)])  77.4 us
    ppermute x1, waiting for transfers between devices, swap_on(): return lax.ppermute(x, ('zh', 'core'), [(s, 2 + s), (2 + s, s)])  50.1 us
    all_to_all x4, blocking collectives, over_y(): return lax.all_to_all(x, 'y', split_axis=0, concat_axis=0, tiled=True)  35.5 us
    all_to_all x2, blocking collectives, over_y_core(): lax.all_to_all(x, ('y', 'core'), split_axis=0, concat_axis=0, tiled=True)  26.2 us
    ppermute x2, waiting for transfers between devices, beside(): found.append(lax.ppermute(x, 'region', ahead + [(b, a) for a, b in ahead]))  18 us
    ppermute x5, waiting for transfers between devices, swap(): return lax.ppermute(x, 'zh', [(0, 1), (1, 0)])  17.6 us
    pallas_call x1, Pallas kernels, shards(): call(analyse_kernel, (f32(HALF, width), f32(64, width), f32(64, width)),...  11.8 us
    ppermute x2, starting transfers between devices, beside(): found.append(lax.ppermute(x, 'region', ahead + [(b, a) for a, b in ahead]))  8.74 us
  transfers between devices with their start and end apart: 11, of which 8 were waited for; matrix products, arithmetic and copies ran while one was open for 1% of the time, Pallas kernels for 0%

profile of v4, /device:TPU:1, one launch (start us, length us, event | category | flops | bytes accessed | tf_op | source)
XLA Modules:
  0.0 273.5 jit_solution(2164243090960500840)
XLA Ops:
  0.0 0.0 copy-start
  0.0 0.0 copy-start.2
  0.0 0.0 copy-start.1
  0.0 1.3 copy-done.1
  1.3 0.2 shard_map.55
  1.5 29.5 %collective-permute-start.2 = (f32[64,1024]{1,0:T(8,128)S(1)}, f32[64,1024]{1,0:T(8,128)S(1)}, u32[]{:S(2)}, u32[]{:S(2)}) collective-permute-start(f32[64,1024]{1,0:T(8,128)S(1)} %get-tuple-element.62), channel_id=1, source_target_pairs={{0,8},{8,0},{1,9},{9,1},{2,10},{10,2},{3,11},{11,3},{4,12},{12,4},... | collective-permute-start | bytes 786440 | tf_op jit(solution)/shard_map/ppermute | solution.py:164
  31.1 0.0 copy-done.2
  31.1 0.7 fusion.5
  32.4 14.3 %conditional.7 = (f32[128,1024]{1,0:T(8,128)S(1)}) conditional(s32[]{:T(128)} %bitcast.10, f32[128,1024]{1,0:T(8,128)S(1)} %get-tuple-element.63, f32[64,1024]{1,0:T(8,128)S(1)} %get-tuple-element.66), branch_computations={%region_4.5_spmd, %region_5.6_spmd} | conditional | flops 131072 | bytes 2621488 | solution.py:196
  32.4 9.5 %all_to_all.45 = f32[4,16,1024]{2,1,0:T(8,128)S(1)} all-to-all(f32[4,16,1024]{2,1,0:T(8,128)S(1)} %bitcast.31), channel_id=1, replica_groups=mesh['region'=64,'zh'=2,'y'=4,'core'=2] {'y'}, dimensions={0} | all-to-all | bytes 524288 | tf_op jit(solution)/shard_map/cond/branch_1_fun/all_to_all | solution.py:173
  41.9 1.3 collective-permute-start
  43.2 3.4 %collective-permute-done = f32[64,1024]{1,0:T(8,128)S(1)} collective-permute-done((f32[64,1024]{1,0:T(8,128)S(1)}, f32[64,1024]{1,0:T(8,128)S(1)}, u32[]{:S(2)}, u32[]{:S(2)}) %collective-permute-start) | collective-permute-done | bytes 262176 | tf_op jit(solution)/shard_map/cond/branch_1_fun/ppermute | solution.py:170
  46.7 5.7 %collective-permute-start.3 = (f32[128,1024]{1,0:T(8,128)S(1)}, f32[128,1024]{1,0:T(8,128)S(1)}, u32[]{:S(2)}, u32[]{:S(2)}) collective-permute-start(f32[128,1024]{1,0:T(8,128)S(1)} %get-tuple-element.95), channel_id=1, source_target_pairs={{1,9},{9,1},{3,11},{11,3},{5,13},{13,5},{7,15},{15,7},{17,25},{25,... | collective-permute-start | bytes 1572872 | tf_op jit(solution)/shard_map/ppermute | solution.py:167
  52.4 0.8 constant_dynamic-slice_fusion
  53.2 0.7 fusion.1
  53.8 11.8 %conditional.6 = (f32[128,1024]{1,0:T(8,128)S(1)}) conditional(s32[]{:T(128)} %bitcast.10, f32[128,1024]{1,0:T(8,128)S(1)} %get-tuple-element.63, f32[128,1024]{1,0:T(8,128)S(1)} %get-tuple-element.63), branch_computations={%region_0.0_spmd, %region_1.0_spmd} | conditional | bytes 2097160 | solution.py:214
  53.9 11.7 %all_to_all.44 = f32[8,16,1024]{2,1,0:T(8,128)S(1)} all-to-all(f32[8,16,1024]{2,1,0:T(8,128)S(1)} %copy.18), channel_id=1, replica_groups=mesh['region'=64,'zh'=2,'y'=4,'core'=2] {'y','core'}, dimensions={0} | all-to-all | bytes 1048576 | tf_op jit(solution)/shard_map/cond/branch_1_fun/all_to_all | solution.py:176
  65.6 0.0 copy-done
  65.6 0.9 select_reduce_fusion.1
  66.6 0.0 collective-permute-done.2
  66.6 13.2 %conditional.8 = (f32[128,1024]{1,0:T(8,128)S(1)}) conditional(s32[]{:T(128)} %bitcast.10, f32[64,1024]{1,0:T(8,128)S(1)} %collective-permute-done.2, f32[64,1024]{1,0:T(8,128)S(1)} %collective-permute-done.2), branch_computations={%region_6.7_spmd, %region_7.8_spmd} | conditional | flops 131072 | bytes 2621488 | solution.py:216
  66.6 7.9 %all_to_all.46 = f32[4,16,1024]{2,1,0:T(8,128)S(1)} all-to-all(f32[4,16,1024]{2,1,0:T(8,128)S(1)} %bitcast.25), channel_id=1, replica_groups=mesh['region'=64,'zh'=2,'y'=4,'core'=2] {'y'}, dimensions={0} | all-to-all | bytes 524288 | tf_op jit(solution)/shard_map/cond/branch_1_fun/all_to_all | solution.py:173
  74.6 4.1 %collective-permute-start.1 = (f32[64,1024]{1,0:T(8,128)S(1)}, f32[64,1024]{1,0:T(8,128)S(1)}, u32[]{:S(2)}, u32[]{:S(2)}) collective-permute-start(f32[64,1024]{1,0:T(8,128)S(1)} %bitcast.28), channel_id=1, source_target_pairs={{1,0},{3,2},{5,4},{7,6},{9,8},{11,10},{13,12},{15,14},{17,16},{19,... | collective-permute-start | bytes 786440 | tf_op jit(solution)/shard_map/cond/branch_1_fun/ppermute | solution.py:170
  78.7 1.1 collective-permute-done.1
  79.8 50.1 %collective-permute-done.3.late_ref = f32[128,1024]{1,0:T(8,128)S(1)} collective-permute-done((f32[128,1024]{1,0:T(8,128)S(1)}, f32[128,1024]{1,0:T(8,128)S(1)}, u32[]{:S(2)}, u32[]{:S(2)}) %collective-permute-start.3) | collective-permute-done | bytes 524320 | tf_op jit(solution)/shard_map/ppermute | solution.py:167
  130.0 2.0 shard_map.56
  131.9 1.9 collective-permute-start.4
  133.9 6.8 %collective-permute-start.5 = (f32[400,128]{1,0:T(8,128)S(1)}, f32[400,128]{1,0:T(8,128)S(1)}, u32[]{:S(2)}, u32[]{:S(2)}) collective-permute-start(f32[400,128]{1,0:T(8,128)S(1)} %get-tuple-element.70.gram_ref), channel_id=1, source_target_pairs={{16,32},{48,64},{80,96},{112,128},{144,160},{176,192},{208,224},{2... | collective-permute-start | bytes 614408 | tf_op jit(solution)/shard_map/ppermute | solution.py:182
  140.7 0.0 collective-permute-done.4.west_ref
  140.7 18.0 %collective-permute-done.5.east_ref = f32[400,128]{1,0:T(8,128)S(1)} collective-permute-done((f32[400,128]{1,0:T(8,128)S(1)}, f32[400,128]{1,0:T(8,128)S(1)}, u32[]{:S(2)}, u32[]{:S(2)}) %collective-permute-start.5) | collective-permute-done | bytes 204832 | tf_op jit(solution)/shard_map/ppermute | solution.py:182
  158.7 11.8 %shard_map.57 = (f32[128,1024]{1,0:T(8,128)S(1)}, f32[64,1024]{1,0:T(8,128)S(1)}, f32[64,1024]{1,0:T(8,128)S(1)}) custom-call(s32[1]{0:T(128)} %bitcast.9.core_ref, f32[400,128]{1,0:T(8,128)S(1)} %get-tuple-element.70.gram_ref, f32[400,128]{1,0:T(8,128)S(1)} %collective-permute-done.4.west_ref, f32[400,128]{1,0:T(8,128)S(1)} %collective-permute-done.5.east_ref, ...), custom_call_target="tpu_custom_call" | custom-call | tf_op jit(solution)/shard_map/pallas_call | solution.py:223
  170.5 1.9 collective-permute-start.6
  172.4 1.5 collective-permute-done.6
  174.0 9.1 %collective-permute-start.7 = (f32[4,8,1024]{2,1,0:T(8,128)S(1)}, f32[4,8,1024]{2,1,0:T(8,128)S(1)}, u32[]{:S(2)}, u32[]{:S(2)}) collective-permute-start(f32[4,8,1024]{2,1,0:T(8,128)S(1)} %get-tuple-element.89), channel_id=1, source_target_pairs={{0,8},{8,0},{1,9},{9,1},{2,10},{10,2},{3,11},{11,3},{4,12},{12,4},... | collective-permute-start | bytes 393224 | tf_op jit(solution)/shard_map/ppermute | solution.py:164
  183.1 10.6 %conditional.9 = (f32[4,24,1024]{2,1,0:T(8,128)S(1)}) conditional(s32[]{:T(128)} %bitcast.10, (f32[4,16,1024]{2,1,0:T(8,128)S(1)}, f32[4,8,1024]{2,1,0:T(8,128)S(1)}) %tuple.71, (f32[4,8,1024]{2,1,0:T(8,128)S(1)}, f32[4,16,1024]{2,1,0:T(8,128)S(1)}) %tuple.72), branch_computations={%region_8.9_spmd, %region_9.10_spmd} | conditional | flops 98304 | bytes 1572872 | solution.py:234
  183.1 10.5 %all_to_all.47 = f32[4,24,1024]{2,1,0:T(8,128)S(1)} all-to-all(f32[4,24,1024]{2,1,0:T(8,128)S(1)} %pad_maximum_fusion.4), channel_id=1, replica_groups=mesh['region'=64,'zh'=2,'y'=4,'core'=2] {'y'}, dimensions={0} | all-to-all | bytes 786432 | tf_op jit(solution)/shard_map/cond/branch_1_fun/all_to_all | solution.py:173
  193.7 15.3 %collective-permute-start.8 = (f32[4,8,1024]{2,1,0:T(8,128)S(1)}, f32[4,8,1024]{2,1,0:T(8,128)S(1)}, u32[]{:S(2)}, u32[]{:S(2)}) collective-permute-start(f32[4,8,1024]{2,1,0:T(8,128)S(1)} %get-tuple-element.87), channel_id=1, source_target_pairs={{0,8},{8,0},{1,9},{9,1},{2,10},{10,2},{3,11},{11,3},{4,12},{12,4},... | collective-permute-start | bytes 393224 | tf_op jit(solution)/shard_map/ppermute | solution.py:164
  209.0 8.4 %collective-permute-start.9 = (f32[4,8,1024]{2,1,0:T(8,128)S(1)}, f32[4,8,1024]{2,1,0:T(8,128)S(1)}, u32[]{:S(2)}, u32[]{:S(2)}) collective-permute-start(f32[4,8,1024]{2,1,0:T(8,128)S(1)} %get-tuple-element.86), channel_id=1, source_target_pairs={{0,8},{8,0},{1,9},{9,1},{2,10},{10,2},{3,11},{11,3},{4,12},{12,4},... | collective-permute-start | bytes 393224 | tf_op jit(solution)/shard_map/ppermute | solution.py:164
  217.3 15.3 %collective-permute-start.10 = (f32[4,8,1024]{2,1,0:T(8,128)S(1)}, f32[4,8,1024]{2,1,0:T(8,128)S(1)}, u32[]{:S(2)}, u32[]{:S(2)}) collective-permute-start(f32[4,8,1024]{2,1,0:T(8,128)S(1)} %get-tuple-element.85), channel_id=1, source_target_pairs={{0,8},{8,0},{1,9},{9,1},{2,10},{10,2},{3,11},{11,3},{4,12},{12,4},... | collective-permute-start | bytes 393224 | tf_op jit(solution)/shard_map/ppermute | solution.py:164
  232.6 14.6 %conditional.10 = (f32[128,1024]{1,0:T(8,128)S(1)}) conditional(s32[]{:T(128)} %bitcast.10, f32[128,1024]{1,0:T(8,128)S(1)} %get-tuple-element.76, f32[128,1024]{1,0:T(8,128)S(1)} %get-tuple-element.76), branch_computations={%region_10.11_spmd, %region_11.12_spmd} | conditional | bytes 2097160 | solution.py:243
  232.7 14.5 %all_to_all.48 = f32[8,16,1024]{2,1,0:T(8,128)S(1)} all-to-all(f32[8,16,1024]{2,1,0:T(8,128)S(1)} %copy.19), channel_id=1, replica_groups=mesh['region'=64,'zh'=2,'y'=4,'core'=2] {'y','core'}, dimensions={0} | all-to-all | bytes 1048576 | tf_op jit(solution)/shard_map/cond/branch_1_fun/all_to_all | solution.py:176
  247.1 0.0 collective-permute-done.7
  247.1 7.5 %conditional.11 = (f32[4,8,1024]{2,1,0:T(8,128)S(1)}) conditional(s32[]{:T(128)} %bitcast.10, f32[4,8,1024]{2,1,0:T(8,128)S(1)} %collective-permute-done.7, f32[4,8,1024]{2,1,0:T(8,128)S(1)} %collective-permute-done.7), branch_computations={%region_12.13_spmd, %region_13.14_spmd} | conditional | bytes 524296 | solution.py:245
  247.2 7.5 %all_to_all.49 = f32[4,8,1024]{2,1,0:T(8,128)S(1)} all-to-all(f32[4,8,1024]{2,1,0:T(8,128)S(1)} %copy.20), channel_id=1, replica_groups=mesh['region'=64,'zh'=2,'y'=4,'core'=2] {'y'}, dimensions={0} | all-to-all | bytes 262144 | tf_op jit(solution)/shard_map/cond/branch_1_fun/all_to_all | solution.py:173
  254.7 10.4 %collective-permute-done.8.b_ref = f32[4,8,1024]{2,1,0:T(8,128)S(1)} collective-permute-done((f32[4,8,1024]{2,1,0:T(8,128)S(1)}, f32[4,8,1024]{2,1,0:T(8,128)S(1)}, u32[]{:S(2)}, u32[]{:S(2)}) %collective-permute-start.8) | collective-permute-done | bytes 131104 | tf_op jit(solution)/shard_map/ppermute | solution.py:164
  265.0 4.1 %collective-permute-done.9.c_ref = f32[4,8,1024]{2,1,0:T(8,128)S(1)} collective-permute-done((f32[4,8,1024]{2,1,0:T(8,128)S(1)}, f32[4,8,1024]{2,1,0:T(8,128)S(1)}, u32[]{:S(2)}, u32[]{:S(2)}) %collective-permute-start.9) | collective-permute-done | bytes 131104 | tf_op jit(solution)/shard_map/ppermute | solution.py:164
  269.2 3.1 %collective-permute-done.10.d_ref = f32[4,8,1024]{2,1,0:T(8,128)S(1)} collective-permute-done((f32[4,8,1024]{2,1,0:T(8,128)S(1)}, f32[4,8,1024]{2,1,0:T(8,128)S(1)}, u32[]{:S(2)}, u32[]{:S(2)}) %collective-permute-start.10) | collective-permute-done | bytes 131104 | tf_op jit(solution)/shard_map/ppermute | solution.py:164
  272.3 1.2 shard_map.58
  (11 shorter events, 0.3 us)
Async XLA Ops:
  0.0 65.6 %copy-start = (s32[16,1024]{1,0:T(8,128)S(1)}, s32[16,1024]{1,0:T(8,128)}, u32[]{:S(2)}) copy-start(s32[16,1024]{1,0:T(8,128)} %param.20) | copy-start | bytes 196612
  0.0 31.0 %copy-start.2 = (s32[16]{0:T(128)S(1)}, s32[16]{0:T(128)}, u32[]{:S(2)}) copy-start(s32[16]{0:T(128)} %param.21) | copy-start | bytes 196
  0.0 1.3 copy-start.1
  1.5 65.1 %collective-permute-start.2 = (f32[64,1024]{1,0:T(8,128)S(1)}, f32[64,1024]{1,0:T(8,128)S(1)}, u32[]{:S(2)}, u32[]{:S(2)}) collective-permute-start(f32[64,1024]{1,0:T(8,128)S(1)} %get-tuple-element.62), channel_id=1, source_target_pairs={{0,8},{8,0},{1,9},{9,1},{2,10},{10,2},{3,11},{11,3},{4,12},{12,4},... | collective-permute-start | bytes 786440 | tf_op jit(solution)/shard_map/ppermute | solution.py:164
  41.9 4.7 %collective-permute-start = (f32[64,1024]{1,0:T(8,128)S(1)}, f32[64,1024]{1,0:T(8,128)S(1)}, u32[]{:S(2)}, u32[]{:S(2)}) collective-permute-start(f32[64,1024]{1,0:T(8,128)S(1)} %bitcast.26), channel_id=1, source_target_pairs={{0,1},{2,3},{4,5},{6,7},{8,9},{10,11},{12,13},{14,15},{16,17},{18,... | collective-permute-start | bytes 786440 | tf_op jit(solution)/shard_map/cond/branch_1_fun/ppermute | solution.py:170
  46.7 83.3 %collective-permute-start.3 = (f32[128,1024]{1,0:T(8,128)S(1)}, f32[128,1024]{1,0:T(8,128)S(1)}, u32[]{:S(2)}, u32[]{:S(2)}) collective-permute-start(f32[128,1024]{1,0:T(8,128)S(1)} %get-tuple-element.95), channel_id=1, source_target_pairs={{1,9},{9,1},{3,11},{11,3},{5,13},{13,5},{7,15},{15,7},{17,25},{25,... | collective-permute-start | bytes 1572872 | tf_op jit(solution)/shard_map/ppermute | solution.py:167
  74.6 5.2 %collective-permute-start.1 = (f32[64,1024]{1,0:T(8,128)S(1)}, f32[64,1024]{1,0:T(8,128)S(1)}, u32[]{:S(2)}, u32[]{:S(2)}) collective-permute-start(f32[64,1024]{1,0:T(8,128)S(1)} %bitcast.28), channel_id=1, source_target_pairs={{1,0},{3,2},{5,4},{7,6},{9,8},{11,10},{13,12},{15,14},{17,16},{19,... | collective-permute-start | bytes 786440 | tf_op jit(solution)/shard_map/cond/branch_1_fun/ppermute | solution.py:170
  131.9 8.8 %collective-permute-start.4 = (f32[400,128]{1,0:T(8,128)S(1)}, f32[400,128]{1,0:T(8,128)S(1)}, u32[]{:S(2)}, u32[]{:S(2)}) collective-permute-start(f32[400,128]{1,0:T(8,128)S(1)} %get-tuple-element.70.gram_ref), channel_id=1, source_target_pairs={{0,16},{32,48},{64,80},{96,112},{128,144},{160,176},{192,208},{224... | collective-permute-start | bytes 614408 | tf_op jit(solution)/shard_map/ppermute | solution.py:182
  133.9 24.8 %collective-permute-start.5 = (f32[400,128]{1,0:T(8,128)S(1)}, f32[400,128]{1,0:T(8,128)S(1)}, u32[]{:S(2)}, u32[]{:S(2)}) collective-permute-start(f32[400,128]{1,0:T(8,128)S(1)} %get-tuple-element.70.gram_ref), channel_id=1, source_target_pairs={{16,32},{48,64},{80,96},{112,128},{144,160},{176,192},{208,224},{2... | collective-permute-start | bytes 614408 | tf_op jit(solution)/shard_map/ppermute | solution.py:182
  170.5 3.4 %collective-permute-start.6 = (f32[64,1024]{1,0:T(8,128)S(1)}, f32[64,1024]{1,0:T(8,128)S(1)}, u32[]{:S(2)}, u32[]{:S(2)}) collective-permute-start(f32[64,1024]{1,0:T(8,128)S(1)} %get-tuple-element.74), channel_id=1, source_target_pairs={{0,1},{1,0},{2,3},{3,2},{4,5},{5,4},{6,7},{7,6},{8,9},{9,8},{10,11... | collective-permute-start | bytes 786440 | tf_op jit(solution)/shard_map/ppermute | solution.py:230
  174.0 73.2 %collective-permute-start.7 = (f32[4,8,1024]{2,1,0:T(8,128)S(1)}, f32[4,8,1024]{2,1,0:T(8,128)S(1)}, u32[]{:S(2)}, u32[]{:S(2)}) collective-permute-start(f32[4,8,1024]{2,1,0:T(8,128)S(1)} %get-tuple-element.89), channel_id=1, source_target_pairs={{0,8},{8,0},{1,9},{9,1},{2,10},{10,2},{3,11},{11,3},{4,12},{12,4},... | collective-permute-start | bytes 393224 | tf_op jit(solution)/shard_map/ppermute | solution.py:164
  193.7 71.3 %collective-permute-start.8 = (f32[4,8,1024]{2,1,0:T(8,128)S(1)}, f32[4,8,1024]{2,1,0:T(8,128)S(1)}, u32[]{:S(2)}, u32[]{:S(2)}) collective-permute-start(f32[4,8,1024]{2,1,0:T(8,128)S(1)} %get-tuple-element.87), channel_id=1, source_target_pairs={{0,8},{8,0},{1,9},{9,1},{2,10},{10,2},{3,11},{11,3},{4,12},{12,4},... | collective-permute-start | bytes 393224 | tf_op jit(solution)/shard_map/ppermute | solution.py:164
  209.0 60.2 %collective-permute-start.9 = (f32[4,8,1024]{2,1,0:T(8,128)S(1)}, f32[4,8,1024]{2,1,0:T(8,128)S(1)}, u32[]{:S(2)}, u32[]{:S(2)}) collective-permute-start(f32[4,8,1024]{2,1,0:T(8,128)S(1)} %get-tuple-element.86), channel_id=1, source_target_pairs={{0,8},{8,0},{1,9},{9,1},{2,10},{10,2},{3,11},{11,3},{4,12},{12,4},... | collective-permute-start | bytes 393224 | tf_op jit(solution)/shard_map/ppermute | solution.py:164
  217.3 55.0 %collective-permute-start.10 = (f32[4,8,1024]{2,1,0:T(8,128)S(1)}, f32[4,8,1024]{2,1,0:T(8,128)S(1)}, u32[]{:S(2)}, u32[]{:S(2)}) collective-permute-start(f32[4,8,1024]{2,1,0:T(8,128)S(1)} %get-tuple-element.85), channel_id=1, source_target_pairs={{0,8},{8,0},{1,9},{9,1},{2,10},{10,2},{3,11},{11,3},{4,12},{12,4},... | collective-permute-start | bytes 393224 | tf_op jit(solution)/shard_map/ppermute | solution.py:164

commit v5 on v3

--- a/solution.py
+++ b/solution.py
@@ -226,13 +226,11 @@
     )(which, gram, west, east, average, deviation)
 
     got = lax.ppermute(send, "core", [(0, 1), (1, 0)])
-    back_0 = swap(jnp.where(core == 0, keep, got))
+    back_0 = swap(over_y(jnp.where(core == 0, keep, got)))
     crossing = lax.cond(always, over_y, lambda x: x, jnp.where(core == 0, got, keep))
     back_1 = swap(crossing)
     crossing, mine = lax.optimization_barrier((crossing, mine))
     mine = lax.cond(always, over_y_core, lambda x: x, mine)
-    back_0, mine = lax.optimization_barrier((back_0, mine))
-    back_0 = lax.cond(always, over_y, lambda x: x, back_0)
     return call(join_kernel, f32(*members.shape), [SMEM] + [VMEM] * 3)(side, mine, back_0, back_1)
 
 

time: 269 us -> 278 us (1.033)
  the two profiles are of different devices: /device:TPU:64 before, /device:TPU:41 now
where the time goes in v5:
time: 278 us; the launch traced here: 277 us
  waiting for transfers between devices  103 us (37%)
  starting transfers between devices  95.3 us (34%)
  blocking collectives  57.5 us (21%)
  Pallas kernels  15.2 us (5%)
  local copies, waits for them, and re-layouts  2.79 us (1%)
    ppermute x3, waiting for transfers between devices, swap(): return lax.ppermute(x, 'zh', [(0, 1), (1, 0)])  91.3 us
    ppermute x3, starting transfers between devices, swap(): return lax.ppermute(x, 'zh', [(0, 1), (1, 0)])  53.8 us
    all_to_all x3, blocking collectives, over_y(): return lax.all_to_all(x, 'y', split_axis=0, concat_axis=0, tiled=True)  31.1 us
    all_to_all x2, blocking collectives, over_y_core(): lax.all_to_all(x, ('y', 'core'), split_axis=0, concat_axis=0, tiled=True)  26.4 us
    ppermute x2, starting transfers between devices, to_core(): return lax.ppermute(x, 'core', [(1 - s, s)])  24.8 us
    pallas_call x1, Pallas kernels, shards(): call(analyse_kernel, (f32(HALF, width), f32(64, width), f32(64, width)),...  11.8 us
    ppermute x2, starting transfers between devices, beside(): found.append(lax.ppermute(x, 'region', ahead + [(b, a) for a, b in ahead]))  6.79 us
    ppermute x2, waiting for transfers between devices, beside(): found.append(lax.ppermute(x, 'region', ahead + [(b, a) for a, b in ahead]))  6.39 us
  transfers between devices with their start and end apart: 10, of which 8 were waited for; matrix products, arithmetic and copies ran while one was open for 1% of the time, Pallas kernels for 0%

profile of v5, /device:TPU:41, one launch (start us, length us, event | category | flops | bytes accessed | tf_op | source)
XLA Modules:
  0.0 277.1 jit_solution(16292764901854646809)
XLA Ops:
  0.0 0.0 copy-start
  0.0 0.0 copy-start.2
  0.0 0.0 copy-start.1
  0.0 1.3 copy-done.1
  1.3 0.2 shard_map.55
  1.5 27.8 %collective-permute-start.2 = (f32[64,1024]{1,0:T(8,128)S(1)}, f32[64,1024]{1,0:T(8,128)S(1)}, u32[]{:S(2)}, u32[]{:S(2)}) collective-permute-start(f32[64,1024]{1,0:T(8,128)S(1)} %get-tuple-element.45), channel_id=1, source_target_pairs={{0,8},{8,0},{1,9},{9,1},{2,10},{10,2},{3,11},{11,3},{4,12},{12,4},... | collective-permute-start | bytes 786440 | tf_op jit(solution)/shard_map/ppermute | solution.py:162
  29.3 0.0 copy-done.2
  29.3 0.6 fusion.3
  30.6 13.2 %conditional.6 = (f32[128,1024]{1,0:T(8,128)S(1)}) conditional(s32[]{:T(128)} %bitcast.11, f32[128,1024]{1,0:T(8,128)S(1)} %get-tuple-element.46, f32[64,1024]{1,0:T(8,128)S(1)} %get-tuple-element.49), branch_computations={%region_4.5_spmd, %region_5.6_spmd} | conditional | flops 131072 | bytes 2621488 | solution.py:194
  30.6 8.8 %all_to_all.58 = f32[4,16,1024]{2,1,0:T(8,128)S(1)} all-to-all(f32[4,16,1024]{2,1,0:T(8,128)S(1)} %bitcast.32), channel_id=1, replica_groups=mesh['region'=64,'zh'=2,'y'=4,'core'=2] {'y'}, dimensions={0} | all-to-all | bytes 524288 | tf_op jit(solution)/shard_map/cond/branch_1_fun/all_to_all | solution.py:171
  39.4 1.3 collective-permute-start
  40.7 3.1 %collective-permute-done = f32[64,1024]{1,0:T(8,128)S(1)} collective-permute-done((f32[64,1024]{1,0:T(8,128)S(1)}, f32[64,1024]{1,0:T(8,128)S(1)}, u32[]{:S(2)}, u32[]{:S(2)}) %collective-permute-start) | collective-permute-done | bytes 262176 | tf_op jit(solution)/shard_map/cond/branch_1_fun/ppermute | solution.py:168
  43.8 1.9 collective-permute-start.3
  45.8 0.8 constant_dynamic-slice_fusion
  46.6 0.6 fusion.1
  47.2 12.1 %conditional.5 = (f32[128,1024]{1,0:T(8,128)S(1)}) conditional(s32[]{:T(128)} %bitcast.11, f32[128,1024]{1,0:T(8,128)S(1)} %get-tuple-element.46, f32[128,1024]{1,0:T(8,128)S(1)} %get-tuple-element.46), branch_computations={%region_0.0_spmd, %region_1.0_spmd} | conditional | bytes 2097160 | solution.py:212
  47.3 12.0 %all_to_all.57 = f32[8,16,1024]{2,1,0:T(8,128)S(1)} all-to-all(f32[8,16,1024]{2,1,0:T(8,128)S(1)} %copy.16), channel_id=1, replica_groups=mesh['region'=64,'zh'=2,'y'=4,'core'=2] {'y','core'}, dimensions={0} | all-to-all | bytes 1048576 | tf_op jit(solution)/shard_map/cond/branch_1_fun/all_to_all | solution.py:174
  59.3 0.0 copy-done
  59.3 0.9 select_reduce_fusion.1
  60.2 27.8 %collective-permute-done.2 = f32[64,1024]{1,0:T(8,128)S(1)} collective-permute-done((f32[64,1024]{1,0:T(8,128)S(1)}, f32[64,1024]{1,0:T(8,128)S(1)}, u32[]{:S(2)}, u32[]{:S(2)}) %collective-permute-start.2) | collective-permute-done | bytes 262176 | tf_op jit(solution)/shard_map/ppermute | solution.py:162
  88.1 38.2 %conditional.7 = (f32[128,1024]{1,0:T(8,128)S(1)}) conditional(s32[]{:T(128)} %bitcast.11, f32[64,1024]{1,0:T(8,128)S(1)} %collective-permute-done.2, f32[64,1024]{1,0:T(8,128)S(1)} %collective-permute-done.2), branch_computations={%region_6.7_spmd, %region_7.8_spmd} | conditional | flops 131072 | bytes 2621488 | solution.py:214
  88.1 13.5 %all_to_all.59 = f32[4,16,1024]{2,1,0:T(8,128)S(1)} all-to-all(f32[4,16,1024]{2,1,0:T(8,128)S(1)} %bitcast.25), channel_id=1, replica_groups=mesh['region'=64,'zh'=2,'y'=4,'core'=2] {'y'}, dimensions={0} | all-to-all | bytes 524288 | tf_op jit(solution)/shard_map/cond/branch_1_fun/all_to_all | solution.py:171
  101.6 23.5 %collective-permute-start.1 = (f32[64,1024]{1,0:T(8,128)S(1)}, f32[64,1024]{1,0:T(8,128)S(1)}, u32[]{:S(2)}, u32[]{:S(2)}) collective-permute-start(f32[64,1024]{1,0:T(8,128)S(1)} %bitcast.30), channel_id=1, source_target_pairs={{1,0},{3,2},{5,4},{7,6},{9,8},{11,10},{13,12},{15,14},{17,16},{19,... | collective-permute-start | bytes 786440 | tf_op jit(solution)/shard_map/cond/branch_1_fun/ppermute | solution.py:168
  125.1 1.1 collective-permute-done.1
  126.3 0.0 collective-permute-done.3.late_ref
  126.3 2.0 shard_map.56
  128.3 3.2 %collective-permute-start.4 = (f32[400,128]{1,0:T(8,128)S(1)}, f32[400,128]{1,0:T(8,128)S(1)}, u32[]{:S(2)}, u32[]{:S(2)}) collective-permute-start(f32[400,128]{1,0:T(8,128)S(1)} %get-tuple-element.53.gram_ref), channel_id=1, source_target_pairs={{0,16},{32,48},{64,80},{96,112},{128,144},{160,176},{192,208},{224... | collective-permute-start | bytes 614408 | tf_op jit(solution)/shard_map/ppermute | solution.py:180
  131.5 3.6 %collective-permute-start.5 = (f32[400,128]{1,0:T(8,128)S(1)}, f32[400,128]{1,0:T(8,128)S(1)}, u32[]{:S(2)}, u32[]{:S(2)}) collective-permute-start(f32[400,128]{1,0:T(8,128)S(1)} %get-tuple-element.53.gram_ref), channel_id=1, source_target_pairs={{16,32},{48,64},{80,96},{112,128},{144,160},{176,192},{208,224},{2... | collective-permute-start | bytes 614408 | tf_op jit(solution)/shard_map/ppermute | solution.py:180
  135.1 1.4 collective-permute-done.4.west_ref
  136.5 5.0 %collective-permute-done.5.east_ref = f32[400,128]{1,0:T(8,128)S(1)} collective-permute-done((f32[400,128]{1,0:T(8,128)S(1)}, f32[400,128]{1,0:T(8,128)S(1)}, u32[]{:S(2)}, u32[]{:S(2)}) %collective-permute-start.5) | collective-permute-done | bytes 204832 | tf_op jit(solution)/shard_map/ppermute | solution.py:180
  141.5 11.8 %shard_map.57 = (f32[128,1024]{1,0:T(8,128)S(1)}, f32[64,1024]{1,0:T(8,128)S(1)}, f32[64,1024]{1,0:T(8,128)S(1)}) custom-call(s32[1]{0:T(128)} %bitcast.12.core_ref, f32[400,128]{1,0:T(8,128)S(1)} %get-tuple-element.53.gram_ref, f32[400,128]{1,0:T(8,128)S(1)} %collective-permute-done.4.west_ref, f32[400,128]{1,0:T(8,128)S(1)} %collective-permute-done.5.east_ref, ...), custom_call_target="tpu_custom_call" | custom-call | tf_op jit(solution)/shard_map/pallas_call | solution.py:221
  153.3 3.4 %collective-permute-start.6 = (f32[64,1024]{1,0:T(8,128)S(1)}, f32[64,1024]{1,0:T(8,128)S(1)}, u32[]{:S(2)}, u32[]{:S(2)}) collective-permute-start(f32[64,1024]{1,0:T(8,128)S(1)} %get-tuple-element.56), channel_id=1, source_target_pairs={{0,1},{1,0},{2,3},{3,2},{4,5},{5,4},{6,7},{7,6},{8,9},{9,8},{10,11... | collective-permute-start | bytes 786440 | tf_op jit(solution)/shard_map/ppermute | solution.py:228
  156.7 1.1 collective-permute-done.6
  157.9 0.8 broadcast_select_fusion
  158.6 8.8 %conditional.8 = (f32[64,1024]{1,0:T(8,128)S(1)}) conditional(s32[]{:T(128)} %bitcast.11, f32[64,1024]{1,0:T(8,128)S(1)} %get-tuple-element.65, f32[64,1024]{1,0:T(8,128)S(1)} %get-tuple-element.65), branch_computations={%region_8.9_spmd, %region_9.10_spmd} | conditional | bytes 1048584 | solution.py:230
  158.7 8.8 %all_to_all.60 = f32[4,16,1024]{2,1,0:T(8,128)S(1)} all-to-all(f32[4,16,1024]{2,1,0:T(8,128)S(1)} %copy.17), channel_id=1, replica_groups=mesh['region'=64,'zh'=2,'y'=4,'core'=2] {'y'}, dimensions={0} | all-to-all | bytes 524288 | tf_op jit(solution)/shard_map/cond/branch_1_fun/all_to_all | solution.py:171
  167.5 4.6 %all-to-all-start.5 = ((f32[4,16,1024]{2,1,0:T(8,128)}), f32[4,16,1024]{2,1,0:T(8,128)S(1)}, u32[]{:S(2)}, u32[]{:S(2)}) async-start(f32[4,16,1024]{2,1,0:T(8,128)} %bitcast.19), calls=%async_computation.5 | async-start | bytes 524288 | tf_op jit(solution)/shard_map/all_to_all | solution.py:171
  172.0 21.6 %collective-permute-start.8 = (f32[64,1024]{1,0:T(8,128)S(1)}, f32[64,1024]{1,0:T(8,128)S(1)}, u32[]{:S(2)}, u32[]{:S(2)}) collective-permute-start(f32[64,1024]{1,0:T(8,128)S(1)} %get-tuple-element.73), channel_id=1, source_target_pairs={{0,8},{8,0},{1,9},{9,1},{2,10},{10,2},{3,11},{11,3},{4,12},{12,4},... | collective-permute-start | bytes 786440 | tf_op jit(solution)/shard_map/ppermute | solution.py:162
  193.7 0.0 all-to-all-done.5
  193.7 4.4 %collective-permute-start.7 = (f32[64,1024]{1,0:T(8,128)S(1)}, f32[64,1024]{1,0:T(8,128)S(1)}, u32[]{:S(2)}, u32[]{:S(2)}) collective-permute-start(f32[64,1024]{1,0:T(8,128)S(1)} %bitcast.33), channel_id=1, source_target_pairs={{0,8},{8,0},{1,9},{9,1},{2,10},{10,2},{3,11},{11,3},{4,12},{12,4},... | collective-permute-start | bytes 786440 | tf_op jit(solution)/shard_map/ppermute | solution.py:162
  198.1 14.4 %conditional.9 = (f32[128,1024]{1,0:T(8,128)S(1)}) conditional(s32[]{:T(128)} %bitcast.11, f32[128,1024]{1,0:T(8,128)S(1)} %get-tuple-element.59, f32[128,1024]{1,0:T(8,128)S(1)} %get-tuple-element.59), branch_computations={%region_10.11_spmd, %region_11.12_spmd} | conditional | bytes 2097160 | solution.py:233
  198.1 14.4 %all_to_all.61 = f32[8,16,1024]{2,1,0:T(8,128)S(1)} all-to-all(f32[8,16,1024]{2,1,0:T(8,128)S(1)} %copy.18), channel_id=1, replica_groups=mesh['region'=64,'zh'=2,'y'=4,'core'=2] {'y','core'}, dimensions={0} | all-to-all | bytes 1048576 | tf_op jit(solution)/shard_map/cond/branch_1_fun/all_to_all | solution.py:174
  212.5 57.8 %collective-permute-done.8.later_ref = f32[64,1024]{1,0:T(8,128)S(1)} collective-permute-done((f32[64,1024]{1,0:T(8,128)S(1)}, f32[64,1024]{1,0:T(8,128)S(1)}, u32[]{:S(2)}, u32[]{:S(2)}) %collective-permute-start.8) | collective-permute-done | bytes 262176 | tf_op jit(solution)/shard_map/ppermute | solution.py:162
  270.3 5.6 %collective-permute-done.7.first_ref = f32[64,1024]{1,0:T(8,128)S(1)} collective-permute-done((f32[64,1024]{1,0:T(8,128)S(1)}, f32[64,1024]{1,0:T(8,128)S(1)}, u32[]{:S(2)}, u32[]{:S(2)}) %collective-permute-start.7) | collective-permute-done | bytes 262176 | tf_op jit(solution)/shard_map/ppermute | solution.py:162
  275.9 1.2 shard_map.58
  (7 shorter events, 0.2 us)
Async XLA Ops:
  0.0 59.3 %copy-start = (s32[16,1024]{1,0:T(8,128)S(1)}, s32[16,1024]{1,0:T(8,128)}, u32[]{:S(2)}) copy-start(s32[16,1024]{1,0:T(8,128)} %param.18) | copy-start | bytes 196612
  0.0 29.3 %copy-start.2 = (s32[16]{0:T(128)S(1)}, s32[16]{0:T(128)}, u32[]{:S(2)}) copy-start(s32[16]{0:T(128)} %param.19) | copy-start | bytes 196
  0.0 1.3 copy-start.1
  1.5 86.6 %collective-permute-start.2 = (f32[64,1024]{1,0:T(8,128)S(1)}, f32[64,1024]{1,0:T(8,128)S(1)}, u32[]{:S(2)}, u32[]{:S(2)}) collective-permute-start(f32[64,1024]{1,0:T(8,128)S(1)} %get-tuple-element.45), channel_id=1, source_target_pairs={{0,8},{8,0},{1,9},{9,1},{2,10},{10,2},{3,11},{11,3},{4,12},{12,4},... | collective-permute-start | bytes 786440 | tf_op jit(solution)/shard_map/ppermute | solution.py:162
  39.4 4.4 %collective-permute-start = (f32[64,1024]{1,0:T(8,128)S(1)}, f32[64,1024]{1,0:T(8,128)S(1)}, u32[]{:S(2)}, u32[]{:S(2)}) collective-permute-start(f32[64,1024]{1,0:T(8,128)S(1)} %bitcast.28), channel_id=1, source_target_pairs={{0,1},{2,3},{4,5},{6,7},{8,9},{10,11},{12,13},{14,15},{16,17},{18,... | collective-permute-start | bytes 786440 | tf_op jit(solution)/shard_map/cond/branch_1_fun/ppermute | solution.py:168
  43.8 82.5 %collective-permute-start.3 = (f32[128,1024]{1,0:T(8,128)S(1)}, f32[128,1024]{1,0:T(8,128)S(1)}, u32[]{:S(2)}, u32[]{:S(2)}) collective-permute-start(f32[128,1024]{1,0:T(8,128)S(1)} %get-tuple-element.71), channel_id=1, source_target_pairs={{1,9},{9,1},{3,11},{11,3},{5,13},{13,5},{7,15},{15,7},{17,25},{25,... | collective-permute-start | bytes 1572872 | tf_op jit(solution)/shard_map/ppermute | solution.py:165
  101.6 24.7 %collective-permute-start.1 = (f32[64,1024]{1,0:T(8,128)S(1)}, f32[64,1024]{1,0:T(8,128)S(1)}, u32[]{:S(2)}, u32[]{:S(2)}) collective-permute-start(f32[64,1024]{1,0:T(8,128)S(1)} %bitcast.30), channel_id=1, source_target_pairs={{1,0},{3,2},{5,4},{7,6},{9,8},{11,10},{13,12},{15,14},{17,16},{19,... | collective-permute-start | bytes 786440 | tf_op jit(solution)/shard_map/cond/branch_1_fun/ppermute | solution.py:168
  128.3 8.2 %collective-permute-start.4 = (f32[400,128]{1,0:T(8,128)S(1)}, f32[400,128]{1,0:T(8,128)S(1)}, u32[]{:S(2)}, u32[]{:S(2)}) collective-permute-start(f32[400,128]{1,0:T(8,128)S(1)} %get-tuple-element.53.gram_ref), channel_id=1, source_target_pairs={{0,16},{32,48},{64,80},{96,112},{128,144},{160,176},{192,208},{224... | collective-permute-start | bytes 614408 | tf_op jit(solution)/shard_map/ppermute | solution.py:180
  131.5 10.0 %collective-permute-start.5 = (f32[400,128]{1,0:T(8,128)S(1)}, f32[400,128]{1,0:T(8,128)S(1)}, u32[]{:S(2)}, u32[]{:S(2)}) collective-permute-start(f32[400,128]{1,0:T(8,128)S(1)} %get-tuple-element.53.gram_ref), channel_id=1, source_target_pairs={{16,32},{48,64},{80,96},{112,128},{144,160},{176,192},{208,224},{2... | collective-permute-start | bytes 614408 | tf_op jit(solution)/shard_map/ppermute | solution.py:180
  153.3 4.6 %collective-permute-start.6 = (f32[64,1024]{1,0:T(8,128)S(1)}, f32[64,1024]{1,0:T(8,128)S(1)}, u32[]{:S(2)}, u32[]{:S(2)}) collective-permute-start(f32[64,1024]{1,0:T(8,128)S(1)} %get-tuple-element.56), channel_id=1, source_target_pairs={{0,1},{1,0},{2,3},{3,2},{4,5},{5,4},{6,7},{7,6},{8,9},{9,8},{10,11... | collective-permute-start | bytes 786440 | tf_op jit(solution)/shard_map/ppermute | solution.py:228
  167.5 26.2 %all-to-all-start.5 = ((f32[4,16,1024]{2,1,0:T(8,128)}), f32[4,16,1024]{2,1,0:T(8,128)S(1)}, u32[]{:S(2)}, u32[]{:S(2)}) async-start(f32[4,16,1024]{2,1,0:T(8,128)} %bitcast.19), calls=%async_computation.5 | async-start | bytes 524288 | tf_op jit(solution)/shard_map/all_to_all | solution.py:171
  172.0 98.3 %collective-permute-start.8 = (f32[64,1024]{1,0:T(8,128)S(1)}, f32[64,1024]{1,0:T(8,128)S(1)}, u32[]{:S(2)}, u32[]{:S(2)}) collective-permute-start(f32[64,1024]{1,0:T(8,128)S(1)} %get-tuple-element.73), channel_id=1, source_target_pairs={{0,8},{8,0},{1,9},{9,1},{2,10},{10,2},{3,11},{11,3},{4,12},{12,4},... | collective-permute-start | bytes 786440 | tf_op jit(solution)/shard_map/ppermute | solution.py:162
  193.7 82.2 %collective-permute-start.7 = (f32[64,1024]{1,0:T(8,128)S(1)}, f32[64,1024]{1,0:T(8,128)S(1)}, u32[]{:S(2)}, u32[]{:S(2)}) collective-permute-start(f32[64,1024]{1,0:T(8,128)S(1)} %bitcast.33), channel_id=1, source_target_pairs={{0,8},{8,0},{1,9},{9,1},{2,10},{10,2},{3,11},{11,3},{4,12},{12,4},... | collective-permute-start | bytes 786440 | tf_op jit(solution)/shard_map/ppermute | solution.py:162

commit v6 on v4

--- a/solution.py
+++ b/solution.py
@@ -18,7 +18,7 @@
 SMEM = pl.BlockSpec(memory_space=pltpu.SMEM)
 
 
-def call(kernel, outs, specs, scratch=()):
+def call(kernel, outs, specs, scratch=(), weight=0):
     return pl.pallas_call(
         kernel,
         out_shape=outs,
@@ -26,7 +26,7 @@
         out_specs=jax.tree.map(lambda _: VMEM, outs),
         scratch_shapes=list(scratch),
         compiler_params=pltpu.CompilerParams(vmem_limit_bytes=24 << 20),
-        cost_estimate=pl.CostEstimate(flops=0, bytes_accessed=0, transcendentals=0),
+        cost_estimate=pl.CostEstimate(flops=weight, bytes_accessed=weight, transcendentals=0),
     )
 
 
@@ -50,7 +50,7 @@
                 own_ref[pl.ds(16 * b, 16), :] = rows(mine + b)
 
 
-def join_kernel(zh_ref, own_ref, a_ref, b_ref, c_ref, d_ref, out_ref):
+def join_first_kernel(zh_ref, own_ref, first_ref, out_ref):
     for side in range(2):
 
         @pl.when(zh_ref[0] == side)
@@ -59,10 +59,19 @@
             for b in range(8):
                 out_ref[:, mine + b, :] = own_ref[pl.ds(16 * b, 16), :]
             for y in range(4):
-                out_ref[0:8, theirs + 2 * y, :] = a_ref[y]
-                out_ref[8:16, theirs + 2 * y, :] = b_ref[y]
-                out_ref[0:8, theirs + 2 * y + 1, :] = c_ref[y]
-                out_ref[8:16, theirs + 2 * y + 1, :] = d_ref[y]
+                out_ref[0:8, theirs + 2 * y, :] = first_ref[y]
+
+
+def join_rest_kernel(zh_ref, rest_ref, begun_ref, out_ref):
+    out_ref[...] = begun_ref[...]
+    for side in range(2):
+
+        @pl.when(zh_ref[0] == side)
+        def _():
+            theirs = 8 * (1 - side)
+            for y in range(4):
+                out_ref[8:16, theirs + 2 * y, :] = rest_ref[y, 0:8]
+                out_ref[:, theirs + 2 * y + 1, :] = rest_ref[y, 8:24]
 
 
 def product(a, b):
@@ -238,12 +247,13 @@
         lower[:, 8:],
         upper,
     )
-    rest = [swap(crossing[:, 8 * k : 8 * k + 8]) for k in range(3)]
+    back_1 = swap(crossing)
     crossing, mine = lax.optimization_barrier((crossing, mine))
     mine = lax.cond(always, over_y_core, lambda x: x, mine)
     back_0, mine = lax.optimization_barrier((back_0, mine))
     back_0 = lax.cond(always, over_y, lambda x: x, back_0)
-    return call(join_kernel, f32(*members.shape), [SMEM] + [VMEM] * 5)(side, mine, back_0, *rest)
+    out = call(join_first_kernel, f32(*members.shape), [SMEM] + [VMEM] * 2, weight=1 << 36)(side, mine, back_0)
+    return call(join_rest_kernel, f32(*members.shape), [SMEM] + [VMEM] * 2)(side, back_1, out)
 
 
 def solution(mesh):

time: 277 us -> 277 us (level)
  waiting for transfers between devices: 91.8 us -> 116 us
  starting transfers between devices: 99.2 us -> 75.6 us
    ppermute x5 -> x3, waiting for transfers between devices: 17.6 us -> 42.4 us  [swap(): return lax.ppermute(x, 'zh', [(0, 1), (1, 0)])]
    ppermute x5 -> x3, starting transfers between devices: 77.4 us -> 53.9 us  [swap(): return lax.ppermute(x, 'zh', [(0, 1), (1, 0)])]
  transfers between devices with their start and end apart: 11 -> 9, of which waited for: 8 -> 6; matrix products, arithmetic and copies ran while one was open for 1% -> 1% of each run, Pallas kernels for 0% -> 0%
where the time goes in v6:
time: 277 us; the launch traced here: 274 us
  waiting for transfers between devices  116 us (42%)
  starting transfers between devices  75.6 us (27%)
  blocking collectives  60.8 us (22%)
  Pallas kernels  15.3 us (6%)
  local copies, waits for them, and re-layouts  2.78 us (1%)
    ppermute x3, starting transfers between devices, swap(): return lax.ppermute(x, 'zh', [(0, 1), (1, 0)])  53.9 us
    ppermute x1, waiting for transfers between devices, swap_on(): return lax.ppermute(x, ('zh', 'core'), [(s, 2 + s), (2 + s, s)])  50.1 us
    ppermute x3, waiting for transfers between devices, swap(): return lax.ppermute(x, 'zh', [(0, 1), (1, 0)])  42.4 us
    all_to_all x4, blocking collectives, over_y(): return lax.all_to_all(x, 'y', split_axis=0, concat_axis=0, tiled=True)  35.5 us
    all_to_all x2, blocking collectives, over_y_core(): lax.all_to_all(x, ('y', 'core'), split_axis=0, concat_axis=0, tiled=True)  25.3 us
    ppermute x2, waiting for transfers between devices, beside(): found.append(lax.ppermute(x, 'region', ahead + [(b, a) for a, b in ahead]))  17.9 us
    pallas_call x1, Pallas kernels, shards(): call(analyse_kernel, (f32(HALF, width), f32(64, width), f32(64, width)),...  11.8 us
    ppermute x2, starting transfers between devices, beside(): found.append(lax.ppermute(x, 'region', ahead + [(b, a) for a, b in ahead]))  8.8 us
  transfers between devices with their start and end apart: 9, of which 6 were waited for; matrix products, arithmetic and copies ran while one was open for 1% of the time, Pallas kernels for 0%

profile of v6, /device:TPU:1, one launch (start us, length us, event | category | flops | bytes accessed | tf_op | source)
XLA Modules:
  0.0 273.8 jit_solution(5758565328865571229)
XLA Ops:
  0.0 0.0 copy-start
  0.0 0.0 copy-start.2
  0.0 0.0 copy-start.1
  0.0 1.3 copy-done.1
  1.3 0.2 shard_map.55
  1.5 29.5 %collective-permute-start.2 = (f32[64,1024]{1,0:T(8,128)S(1)}, f32[64,1024]{1,0:T(8,128)S(1)}, u32[]{:S(2)}, u32[]{:S(2)}) collective-permute-start(f32[64,1024]{1,0:T(8,128)S(1)} %get-tuple-element.62), channel_id=1, source_target_pairs={{0,8},{8,0},{1,9},{9,1},{2,10},{10,2},{3,11},{11,3},{4,12},{12,4},... | collective-permute-start | bytes 786440 | tf_op jit(solution)/shard_map/ppermute | solution.py:173
  31.1 0.0 copy-done.2
  31.1 0.6 fusion.4
  32.4 14.3 %conditional.7 = (f32[128,1024]{1,0:T(8,128)S(1)}) conditional(s32[]{:T(128)} %bitcast.9, f32[128,1024]{1,0:T(8,128)S(1)} %get-tuple-element.63, f32[64,1024]{1,0:T(8,128)S(1)} %get-tuple-element.66), branch_computations={%region_4.5_spmd, %region_5.6_spmd} | conditional | flops 131072 | bytes 2621488 | solution.py:205
  32.4 9.5 %all_to_all.45 = f32[4,16,1024]{2,1,0:T(8,128)S(1)} all-to-all(f32[4,16,1024]{2,1,0:T(8,128)S(1)} %bitcast.31), channel_id=1, replica_groups=mesh['region'=64,'zh'=2,'y'=4,'core'=2] {'y'}, dimensions={0} | all-to-all | bytes 524288 | tf_op jit(solution)/shard_map/cond/branch_1_fun/all_to_all | solution.py:182
  41.9 1.3 collective-permute-start
  43.2 3.4 %collective-permute-done = f32[64,1024]{1,0:T(8,128)S(1)} collective-permute-done((f32[64,1024]{1,0:T(8,128)S(1)}, f32[64,1024]{1,0:T(8,128)S(1)}, u32[]{:S(2)}, u32[]{:S(2)}) %collective-permute-start) | collective-permute-done | bytes 262176 | tf_op jit(solution)/shard_map/cond/branch_1_fun/ppermute | solution.py:179
  46.6 5.7 %collective-permute-start.3 = (f32[128,1024]{1,0:T(8,128)S(1)}, f32[128,1024]{1,0:T(8,128)S(1)}, u32[]{:S(2)}, u32[]{:S(2)}) collective-permute-start(f32[128,1024]{1,0:T(8,128)S(1)} %get-tuple-element.92), channel_id=1, source_target_pairs={{1,9},{9,1},{3,11},{11,3},{5,13},{13,5},{7,15},{15,7},{17,25},{25,... | collective-permute-start | bytes 1572872 | tf_op jit(solution)/shard_map/ppermute | solution.py:176
  52.3 0.8 constant_dynamic-slice_fusion
  53.1 0.6 fusion.1
  53.7 11.8 %conditional.6 = (f32[128,1024]{1,0:T(8,128)S(1)}) conditional(s32[]{:T(128)} %bitcast.9, f32[128,1024]{1,0:T(8,128)S(1)} %get-tuple-element.63, f32[128,1024]{1,0:T(8,128)S(1)} %get-tuple-element.63), branch_computations={%region_0.0_spmd, %region_1.0_spmd} | conditional | bytes 2097160 | solution.py:223
  53.8 11.7 %all_to_all.44 = f32[8,16,1024]{2,1,0:T(8,128)S(1)} all-to-all(f32[8,16,1024]{2,1,0:T(8,128)S(1)} %copy.18), channel_id=1, replica_groups=mesh['region'=64,'zh'=2,'y'=4,'core'=2] {'y','core'}, dimensions={0} | all-to-all | bytes 1048576 | tf_op jit(solution)/shard_map/cond/branch_1_fun/all_to_all | solution.py:185
  65.5 0.0 copy-done
  65.5 0.9 select_reduce_fusion.1
  66.5 0.0 collective-permute-done.2
  66.5 13.2 %conditional.8 = (f32[128,1024]{1,0:T(8,128)S(1)}) conditional(s32[]{:T(128)} %bitcast.9, f32[64,1024]{1,0:T(8,128)S(1)} %collective-permute-done.2, f32[64,1024]{1,0:T(8,128)S(1)} %collective-permute-done.2), branch_computations={%region_6.7_spmd, %region_7.8_spmd} | conditional | flops 131072 | bytes 2621488 | solution.py:225
  66.5 7.9 %all_to_all.46 = f32[4,16,1024]{2,1,0:T(8,128)S(1)} all-to-all(f32[4,16,1024]{2,1,0:T(8,128)S(1)} %bitcast.23), channel_id=1, replica_groups=mesh['region'=64,'zh'=2,'y'=4,'core'=2] {'y'}, dimensions={0} | all-to-all | bytes 524288 | tf_op jit(solution)/shard_map/cond/branch_1_fun/all_to_all | solution.py:182
  74.5 4.1 %collective-permute-start.1 = (f32[64,1024]{1,0:T(8,128)S(1)}, f32[64,1024]{1,0:T(8,128)S(1)}, u32[]{:S(2)}, u32[]{:S(2)}) collective-permute-start(f32[64,1024]{1,0:T(8,128)S(1)} %bitcast.26), channel_id=1, source_target_pairs={{1,0},{3,2},{5,4},{7,6},{9,8},{11,10},{13,12},{15,14},{17,16},{19,... | collective-permute-start | bytes 786440 | tf_op jit(solution)/shard_map/cond/branch_1_fun/ppermute | solution.py:179
  78.6 1.1 collective-permute-done.1
  79.7 50.1 %collective-permute-done.3.late_ref = f32[128,1024]{1,0:T(8,128)S(1)} collective-permute-done((f32[128,1024]{1,0:T(8,128)S(1)}, f32[128,1024]{1,0:T(8,128)S(1)}, u32[]{:S(2)}, u32[]{:S(2)}) %collective-permute-start.3) | collective-permute-done | bytes 524320 | tf_op jit(solution)/shard_map/ppermute | solution.py:176
  129.9 2.0 shard_map.56
  131.8 1.9 collective-permute-start.4
  133.8 6.9 %collective-permute-start.5 = (f32[400,128]{1,0:T(8,128)S(1)}, f32[400,128]{1,0:T(8,128)S(1)}, u32[]{:S(2)}, u32[]{:S(2)}) collective-permute-start(f32[400,128]{1,0:T(8,128)S(1)} %get-tuple-element.70.gram_ref), channel_id=1, source_target_pairs={{16,32},{48,64},{80,96},{112,128},{144,160},{176,192},{208,224},{2... | collective-permute-start | bytes 614408 | tf_op jit(solution)/shard_map/ppermute | solution.py:191
  140.6 0.0 collective-permute-done.4.west_ref
  140.7 17.9 %collective-permute-done.5.east_ref = f32[400,128]{1,0:T(8,128)S(1)} collective-permute-done((f32[400,128]{1,0:T(8,128)S(1)}, f32[400,128]{1,0:T(8,128)S(1)}, u32[]{:S(2)}, u32[]{:S(2)}) %collective-permute-start.5) | collective-permute-done | bytes 204832 | tf_op jit(solution)/shard_map/ppermute | solution.py:191
  158.6 11.8 %shard_map.57 = (f32[128,1024]{1,0:T(8,128)S(1)}, f32[64,1024]{1,0:T(8,128)S(1)}, f32[64,1024]{1,0:T(8,128)S(1)}) custom-call(s32[1]{0:T(128)} %bitcast.10.core_ref, f32[400,128]{1,0:T(8,128)S(1)} %get-tuple-element.70.gram_ref, f32[400,128]{1,0:T(8,128)S(1)} %collective-permute-done.4.west_ref, f32[400,128]{1,0:T(8,128)S(1)} %collective-permute-done.5.east_ref, ...), custom_call_target="tpu_custom_call" | custom-call | tf_op jit(solution)/shard_map/pallas_call | solution.py:232
  170.4 1.9 collective-permute-start.6
  172.3 1.5 collective-permute-done.6
  173.9 9.2 %collective-permute-start.8 = (f32[4,8,1024]{2,1,0:T(8,128)S(1)}, f32[4,8,1024]{2,1,0:T(8,128)S(1)}, u32[]{:S(2)}, u32[]{:S(2)}) collective-permute-start(f32[4,8,1024]{2,1,0:T(8,128)S(1)} %get-tuple-element.85), channel_id=1, source_target_pairs={{0,8},{8,0},{1,9},{9,1},{2,10},{10,2},{3,11},{11,3},{4,12},{12,4},... | collective-permute-start | bytes 393224 | tf_op jit(solution)/shard_map/ppermute | solution.py:173
  183.1 10.6 %conditional.9 = (f32[4,24,1024]{2,1,0:T(8,128)S(1)}) conditional(s32[]{:T(128)} %bitcast.9, (f32[4,16,1024]{2,1,0:T(8,128)S(1)}, f32[4,8,1024]{2,1,0:T(8,128)S(1)}) %tuple.69, (f32[4,8,1024]{2,1,0:T(8,128)S(1)}, f32[4,16,1024]{2,1,0:T(8,128)S(1)}) %tuple.70), branch_computations={%region_8.9_spmd, %region_9.10_spmd} | conditional | flops 98304 | bytes 1572872 | solution.py:243
  183.1 10.5 %all_to_all.47 = f32[4,24,1024]{2,1,0:T(8,128)S(1)} all-to-all(f32[4,24,1024]{2,1,0:T(8,128)S(1)} %pad_maximum_fusion.4), channel_id=1, replica_groups=mesh['region'=64,'zh'=2,'y'=4,'core'=2] {'y'}, dimensions={0} | all-to-all | bytes 786432 | tf_op jit(solution)/shard_map/cond/branch_1_fun/all_to_all | solution.py:182
  193.7 15.2 %collective-permute-start.7 = (f32[4,24,1024]{2,1,0:T(8,128)S(1)}, f32[4,24,1024]{2,1,0:T(8,128)S(1)}, u32[]{:S(2)}, u32[]{:S(2)}) collective-permute-start(f32[4,24,1024]{2,1,0:T(8,128)S(1)} %get-tuple-element.94), channel_id=1, source_target_pairs={{0,8},{8,0},{1,9},{9,1},{2,10},{10,2},{3,11},{11,3},{4,12},{12,4},... | collective-permute-start | bytes 1179656 | tf_op jit(solution)/shard_map/ppermute | solution.py:173
  208.9 13.7 %conditional.10 = (f32[128,1024]{1,0:T(8,128)S(1)}) conditional(s32[]{:T(128)} %bitcast.9, f32[128,1024]{1,0:T(8,128)S(1)} %get-tuple-element.76, f32[128,1024]{1,0:T(8,128)S(1)} %get-tuple-element.76), branch_computations={%region_10.11_spmd, %region_11.12_spmd} | conditional | bytes 2097160 | solution.py:252
  208.9 13.6 %all_to_all.48 = f32[8,16,1024]{2,1,0:T(8,128)S(1)} all-to-all(f32[8,16,1024]{2,1,0:T(8,128)S(1)} %copy.19), channel_id=1, replica_groups=mesh['region'=64,'zh'=2,'y'=4,'core'=2] {'y','core'}, dimensions={0} | all-to-all | bytes 1048576 | tf_op jit(solution)/shard_map/cond/branch_1_fun/all_to_all | solution.py:185
  222.6 0.0 collective-permute-done.8
  222.6 7.5 %conditional.11 = (f32[4,8,1024]{2,1,0:T(8,128)S(1)}) conditional(s32[]{:T(128)} %bitcast.9, f32[4,8,1024]{2,1,0:T(8,128)S(1)} %collective-permute-done.8, f32[4,8,1024]{2,1,0:T(8,128)S(1)} %collective-permute-done.8), branch_computations={%region_12.13_spmd, %region_13.14_spmd} | conditional | bytes 524296 | solution.py:254
  222.6 7.5 %all_to_all.49 = f32[4,8,1024]{2,1,0:T(8,128)S(1)} all-to-all(f32[4,8,1024]{2,1,0:T(8,128)S(1)} %copy.20), channel_id=1, replica_groups=mesh['region'=64,'zh'=2,'y'=4,'core'=2] {'y'}, dimensions={0} | all-to-all | bytes 262144 | tf_op jit(solution)/shard_map/cond/branch_1_fun/all_to_all | solution.py:182
  230.1 0.2 shard_map.58.begun_ref
  230.3 42.4 %collective-permute-done.7.rest_ref = f32[4,24,1024]{2,1,0:T(8,128)S(1)} collective-permute-done((f32[4,24,1024]{2,1,0:T(8,128)S(1)}, f32[4,24,1024]{2,1,0:T(8,128)S(1)}, u32[]{:S(2)}, u32[]{:S(2)}) %collective-permute-start.7) | collective-permute-done | bytes 393248 | tf_op jit(solution)/shard_map/ppermute | solution.py:173
  272.7 1.1 shard_map.59
  (10 shorter events, 0.3 us)
Async XLA Ops:
  0.0 65.5 %copy-start = (s32[16,1024]{1,0:T(8,128)S(1)}, s32[16,1024]{1,0:T(8,128)}, u32[]{:S(2)}) copy-start(s32[16,1024]{1,0:T(8,128)} %param.20) | copy-start | bytes 196612
  0.0 31.0 %copy-start.2 = (s32[16]{0:T(128)S(1)}, s32[16]{0:T(128)}, u32[]{:S(2)}) copy-start(s32[16]{0:T(128)} %param.21) | copy-start | bytes 196
  0.0 1.3 copy-start.1
  1.5 65.0 %collective-permute-start.2 = (f32[64,1024]{1,0:T(8,128)S(1)}, f32[64,1024]{1,0:T(8,128)S(1)}, u32[]{:S(2)}, u32[]{:S(2)}) collective-permute-start(f32[64,1024]{1,0:T(8,128)S(1)} %get-tuple-element.62), channel_id=1, source_target_pairs={{0,8},{8,0},{1,9},{9,1},{2,10},{10,2},{3,11},{11,3},{4,12},{12,4},... | collective-permute-start | bytes 786440 | tf_op jit(solution)/shard_map/ppermute | solution.py:173
  41.9 4.7 %collective-permute-start = (f32[64,1024]{1,0:T(8,128)S(1)}, f32[64,1024]{1,0:T(8,128)S(1)}, u32[]{:S(2)}, u32[]{:S(2)}) collective-permute-start(f32[64,1024]{1,0:T(8,128)S(1)} %bitcast.24), channel_id=1, source_target_pairs={{0,1},{2,3},{4,5},{6,7},{8,9},{10,11},{12,13},{14,15},{16,17},{18,... | collective-permute-start | bytes 786440 | tf_op jit(solution)/shard_map/cond/branch_1_fun/ppermute | solution.py:179
  46.6 83.3 %collective-permute-start.3 = (f32[128,1024]{1,0:T(8,128)S(1)}, f32[128,1024]{1,0:T(8,128)S(1)}, u32[]{:S(2)}, u32[]{:S(2)}) collective-permute-start(f32[128,1024]{1,0:T(8,128)S(1)} %get-tuple-element.92), channel_id=1, source_target_pairs={{1,9},{9,1},{3,11},{11,3},{5,13},{13,5},{7,15},{15,7},{17,25},{25,... | collective-permute-start | bytes 1572872 | tf_op jit(solution)/shard_map/ppermute | solution.py:176
  74.5 5.2 %collective-permute-start.1 = (f32[64,1024]{1,0:T(8,128)S(1)}, f32[64,1024]{1,0:T(8,128)S(1)}, u32[]{:S(2)}, u32[]{:S(2)}) collective-permute-start(f32[64,1024]{1,0:T(8,128)S(1)} %bitcast.26), channel_id=1, source_target_pairs={{1,0},{3,2},{5,4},{7,6},{9,8},{11,10},{13,12},{15,14},{17,16},{19,... | collective-permute-start | bytes 786440 | tf_op jit(solution)/shard_map/cond/branch_1_fun/ppermute | solution.py:179
  131.8 8.8 %collective-permute-start.4 = (f32[400,128]{1,0:T(8,128)S(1)}, f32[400,128]{1,0:T(8,128)S(1)}, u32[]{:S(2)}, u32[]{:S(2)}) collective-permute-start(f32[400,128]{1,0:T(8,128)S(1)} %get-tuple-element.70.gram_ref), channel_id=1, source_target_pairs={{0,16},{32,48},{64,80},{96,112},{128,144},{160,176},{192,208},{224... | collective-permute-start | bytes 614408 | tf_op jit(solution)/shard_map/ppermute | solution.py:191
  133.8 24.8 %collective-permute-start.5 = (f32[400,128]{1,0:T(8,128)S(1)}, f32[400,128]{1,0:T(8,128)S(1)}, u32[]{:S(2)}, u32[]{:S(2)}) collective-permute-start(f32[400,128]{1,0:T(8,128)S(1)} %get-tuple-element.70.gram_ref), channel_id=1, source_target_pairs={{16,32},{48,64},{80,96},{112,128},{144,160},{176,192},{208,224},{2... | collective-permute-start | bytes 614408 | tf_op jit(solution)/shard_map/ppermute | solution.py:191
  170.4 3.4 %collective-permute-start.6 = (f32[64,1024]{1,0:T(8,128)S(1)}, f32[64,1024]{1,0:T(8,128)S(1)}, u32[]{:S(2)}, u32[]{:S(2)}) collective-permute-start(f32[64,1024]{1,0:T(8,128)S(1)} %get-tuple-element.73), channel_id=1, source_target_pairs={{0,1},{1,0},{2,3},{3,2},{4,5},{5,4},{6,7},{7,6},{8,9},{9,8},{10,11... | collective-permute-start | bytes 786440 | tf_op jit(solution)/shard_map/ppermute | solution.py:239
  173.9 48.7 %collective-permute-start.8 = (f32[4,8,1024]{2,1,0:T(8,128)S(1)}, f32[4,8,1024]{2,1,0:T(8,128)S(1)}, u32[]{:S(2)}, u32[]{:S(2)}) collective-permute-start(f32[4,8,1024]{2,1,0:T(8,128)S(1)} %get-tuple-element.85), channel_id=1, source_target_pairs={{0,8},{8,0},{1,9},{9,1},{2,10},{10,2},{3,11},{11,3},{4,12},{12,4},... | collective-permute-start | bytes 393224 | tf_op jit(solution)/shard_map/ppermute | solution.py:173
  193.7 79.0 %collective-permute-start.7 = (f32[4,24,1024]{2,1,0:T(8,128)S(1)}, f32[4,24,1024]{2,1,0:T(8,128)S(1)}, u32[]{:S(2)}, u32[]{:S(2)}) collective-permute-start(f32[4,24,1024]{2,1,0:T(8,128)S(1)} %get-tuple-element.94), channel_id=1, source_target_pairs={{0,8},{8,0},{1,9},{9,1},{2,10},{10,2},{3,11},{11,3},{4,12},{12,4},... | collective-permute-start | bytes 1179656 | tf_op jit(solution)/shard_map/ppermute | solution.py:173

commit v7 on v3

--- a/solution.py
+++ b/solution.py
@@ -34,20 +34,14 @@
     return jax.ShapeDtypeStruct(shape, jnp.float32)
 
 
-def split_kernel(zh_ref, x_ref, first_ref, own_ref, later_ref):
-    def rows(band):
-        return x_ref[:, band, :]
-
+def split_kernel(zh_ref, x_ref, own_ref, other_ref):
     for side in range(2):
 
         @pl.when(zh_ref[0] == side)
         def _():
-            mine, theirs = 8 * side, 8 * (1 - side)
-            for y in range(4):
-                first_ref[pl.ds(16 * y, 16), :] = rows(theirs + 2 * y)
-                later_ref[pl.ds(16 * y, 16), :] = rows(theirs + 2 * y + 1)
             for b in range(8):
-                own_ref[pl.ds(16 * b, 16), :] = rows(mine + b)
+                other_ref[pl.ds(16 * b, 16), :] = x_ref[:, 8 * (1 - side) + b, :]
+                own_ref[pl.ds(16 * b, 16), :] = x_ref[:, 8 * side + b, :]
 
 
 def join_kernel(zh_ref, own_ref, first_ref, later_ref, out_ref):
@@ -73,9 +67,9 @@
     )
 
 
-def gram_kernel(core_ref, table_ref, own_ref, early_ref, late_ref, gram_ref, average_ref, deviation_ref):
-    other = jnp.where(core_ref[0] == 0, early_ref[...], late_ref[...])
-    states = jnp.concatenate([own_ref[...], other], axis=0)
+def gram_kernel(table_ref, own_ref, other_ref, gram_ref, average_ref, deviation_ref):
+    other = [other_ref[pl.ds(16 * (2 * y + core), 16), :] for core in range(2) for y in range(4)]
+    states = jnp.concatenate([own_ref[...]] + other, axis=0)
     average = jnp.sum(states, axis=0, keepdims=True) / K
     deviation = states - average
     average_ref[...] = jnp.broadcast_to(average, average_ref.shape)
@@ -154,18 +148,10 @@
     side = zh.astype(jnp.int32).reshape(1)
     which = core.astype(jnp.int32).reshape(1)
 
-    first, own, later = call(
-        split_kernel, (f32(64, width), f32(128, width), f32(64, width)), [SMEM, VMEM]
-    )(side, members)
+    own, other = call(split_kernel, (f32(HALF, width), f32(HALF, width)), [SMEM, VMEM])(side, members)
 
     def swap(x):
         return lax.ppermute(x, "zh", [(0, 1), (1, 0)])
-
-    def swap_on(x, s):
-        return lax.ppermute(x, ("zh", "core"), [(s, 2 + s), (2 + s, s)])
-
-    def to_core(x, s):
-        return lax.ppermute(x, "core", [(1 - s, s)])
 
     def over_y(x):
         return lax.all_to_all(x, "y", split_axis=0, concat_axis=0, tiled=True)
@@ -180,19 +166,8 @@
             found.append(lax.ppermute(x, "region", ahead + [(b, a) for a, b in ahead]))
         return found
 
-    crossed = swap(first)
+    crossed = swap(other)
     always = obs_count[0] > 0
-
-    def spread(later, own):
-        near = over_y(later)
-        far = to_core(near, 1)
-        return jnp.concatenate([far, near]).reshape(HALF, width)
-
-    def no_spread(later, own):
-        return own.reshape(HALF, width)
-
-    later = lax.cond(always, spread, no_spread, later, own)
-    later_crossed = swap_on(later, 1)
 
     band = zh * 8 + y * 2 + core
     pick = lambda t: lax.dynamic_index_in_dim(t, band, 0, keepdims=False)
@@ -204,19 +179,13 @@
     pull = jnp.sum(jnp.where(hit, (accuracy * observed)[:, None], 0.0), axis=0)
     table = jnp.stack([weight, pull])
 
-    def gathered(crossed):
-        near = over_y(crossed)
-        far = to_core(near, 0)
-        return jnp.concatenate([near, far]).reshape(HALF, width)
-
     own = lax.cond(always, over_y_core, lambda x: x, own)
     crossed, own, table = lax.optimization_barrier((crossed, own, table))
-    early = lax.cond(always, gathered, lambda x: jnp.concatenate([x, x]).reshape(HALF, width), crossed)
-    later_crossed, early = lax.optimization_barrier((later_crossed, early))
+    other = over_y_core(crossed)
 
     gram, average, deviation = call(
-        gram_kernel, (f32(400, 128), f32(8, width), f32(K, width)), [SMEM] + [VMEM] * 4
-    )(which, table, own, early, later_crossed)
+        gram_kernel, (f32(400, 128), f32(8, width), f32(K, width)), [VMEM] * 3
+    )(table, own, other)
     west, east = beside(gram)
     mine, keep, send = call(
         analyse_kernel,

time: 269 us -> 271 us (level)
  the two profiles are of different devices: /device:TPU:64 before, /device:TPU:193 now
where the time goes in v7:
time: 271 us
  waiting for transfers between devices  125 us (46%)
  starting transfers between devices  65.8 us (24%)
  blocking collectives  59.4 us (22%)
  Pallas kernels  15.2 us (6%)
  local copies, waits for them, and re-layouts  2.79 us (1%)
    ppermute x3, waiting for transfers between devices, swap(): return lax.ppermute(x, 'zh', [(0, 1), (1, 0)])  120 us
    ppermute x3, starting transfers between devices, swap(): return lax.ppermute(x, 'zh', [(0, 1), (1, 0)])  46.6 us
    all_to_all x3, blocking collectives, over_y_core(): lax.all_to_all(x, ('y', 'core'), split_axis=0, concat_axis=0, tiled=True)  43.2 us
    all_to_all x2, blocking collectives, over_y(): return lax.all_to_all(x, 'y', split_axis=0, concat_axis=0, tiled=True)  16.1 us
    ppermute x2, starting transfers between devices, beside(): found.append(lax.ppermute(x, 'region', ahead + [(b, a) for a, b in ahead]))  15.3 us
    pallas_call x1, Pallas kernels, shards(): call(analyse_kernel, (f32(HALF, width), f32(64, width), f32(64, width)),...  11.8 us
  transfers between devices with their start and end apart: 6, of which 4 were waited for; matrix products, arithmetic and copies ran while one was open for 1% of the time, Pallas kernels for 0%

profile of v7, /device:TPU:193, one launch (start us, length us, event | category | flops | bytes accessed | tf_op | source)
XLA Modules:
  0.0 270.7 jit_solution(4768809777123301794)
XLA Ops:
  0.0 0.0 copy-start
  0.0 0.0 copy-start.2
  0.0 0.0 copy-start.1
  0.0 1.3 copy-done.1
  1.3 0.2 shard_map.55
  1.5 22.1 %collective-permute-start = (f32[128,1024]{1,0:T(8,128)S(1)}, f32[128,1024]{1,0:T(8,128)S(1)}, u32[]{:S(2)}, u32[]{:S(2)}) collective-permute-start(f32[128,1024]{1,0:T(8,128)S(1)} %get-tuple-element.39), channel_id=1, source_target_pairs={{0,8},{8,0},{1,9},{9,1},{2,10},{10,2},{3,11},{11,3},{4,12},{12,4},... | collective-permute-start | bytes 1572872 | tf_op jit(solution)/shard_map/ppermute | solution.py:154
  23.6 0.0 copy-done.2
  23.6 0.6 fusion.3
  24.2 0.8 constant_dynamic-slice_fusion
  25.0 0.6 fusion.1
  26.2 14.9 %conditional.4 = (f32[128,1024]{1,0:T(8,128)S(1)}) conditional(s32[]{:T(128)} %bitcast.10, f32[128,1024]{1,0:T(8,128)S(1)} %get-tuple-element.40, f32[128,1024]{1,0:T(8,128)S(1)} %get-tuple-element.40), branch_computations={%region_0.1_spmd, %region_1.2_spmd} | conditional | bytes 2097160 | solution.py:182
  26.3 14.9 %all_to_all.47 = f32[8,16,1024]{2,1,0:T(8,128)S(1)} all-to-all(f32[8,16,1024]{2,1,0:T(8,128)S(1)} %copy.14), channel_id=1, replica_groups=mesh['region'=64,'zh'=2,'y'=4,'core'=2] {'y','core'}, dimensions={0} | all-to-all | bytes 1048576 | tf_op jit(solution)/shard_map/cond/branch_1_fun/all_to_all | solution.py:160
  41.2 0.0 copy-done
  41.2 0.9 select_reduce_fusion.1
  42.1 47.5 %collective-permute-done = f32[128,1024]{1,0:T(8,128)S(1)} collective-permute-done((f32[128,1024]{1,0:T(8,128)S(1)}, f32[128,1024]{1,0:T(8,128)S(1)}, u32[]{:S(2)}, u32[]{:S(2)}) %collective-permute-start) | collective-permute-done | bytes 524320 | tf_op jit(solution)/shard_map/ppermute | solution.py:154
  89.6 15.1 %all_to_all.51 = f32[8,16,1024]{2,1,0:T(8,128)S(1)} all-to-all(f32[8,16,1024]{2,1,0:T(8,128)S(1)} %bitcast.28), channel_id=1, replica_groups=mesh['region'=64,'zh'=2,'y'=4,'core'=2] {'y','core'}, dimensions={0} | all-to-all | bytes 1048576 | tf_op jit(solution)/shard_map/all_to_all | solution.py:160
  104.7 1.9 shard_map.56
  106.6 3.1 %collective-permute-start.1 = (f32[400,128]{1,0:T(8,128)S(1)}, f32[400,128]{1,0:T(8,128)S(1)}, u32[]{:S(2)}, u32[]{:S(2)}) collective-permute-start(f32[400,128]{1,0:T(8,128)S(1)} %get-tuple-element.44.gram_ref), channel_id=1, source_target_pairs={{0,16},{32,48},{64,80},{96,112},{128,144},{160,176},{192,208},{224... | collective-permute-start | bytes 614408 | tf_op jit(solution)/shard_map/ppermute | solution.py:166
  109.8 12.2 %collective-permute-start.2 = (f32[400,128]{1,0:T(8,128)S(1)}, f32[400,128]{1,0:T(8,128)S(1)}, u32[]{:S(2)}, u32[]{:S(2)}) collective-permute-start(f32[400,128]{1,0:T(8,128)S(1)} %get-tuple-element.44.gram_ref), channel_id=1, source_target_pairs={{16,32},{48,64},{80,96},{112,128},{144,160},{176,192},{208,224},{2... | collective-permute-start | bytes 614408 | tf_op jit(solution)/shard_map/ppermute | solution.py:166
  122.0 0.0 collective-permute-done.1.west_ref
  122.0 4.0 %collective-permute-done.2.east_ref = f32[400,128]{1,0:T(8,128)S(1)} collective-permute-done((f32[400,128]{1,0:T(8,128)S(1)}, f32[400,128]{1,0:T(8,128)S(1)}, u32[]{:S(2)}, u32[]{:S(2)}) %collective-permute-start.2) | collective-permute-done | bytes 204832 | tf_op jit(solution)/shard_map/ppermute | solution.py:166
  126.0 11.8 %shard_map.57 = (f32[128,1024]{1,0:T(8,128)S(1)}, f32[64,1024]{1,0:T(8,128)S(1)}, f32[64,1024]{1,0:T(8,128)S(1)}) custom-call(s32[1]{0:T(128)} %bitcast.9.core_ref, f32[400,128]{1,0:T(8,128)S(1)} %get-tuple-element.44.gram_ref, f32[400,128]{1,0:T(8,128)S(1)} %collective-permute-done.1.west_ref, f32[400,128]{1,0:T(8,128)S(1)} %collective-permute-done.2.east_ref, ...), custom_call_target="tpu_custom_call" | custom-call | tf_op jit(solution)/shard_map/pallas_call | solution.py:190
  137.8 3.9 %collective-permute-start.3 = (f32[64,1024]{1,0:T(8,128)S(1)}, f32[64,1024]{1,0:T(8,128)S(1)}, u32[]{:S(2)}, u32[]{:S(2)}) collective-permute-start(f32[64,1024]{1,0:T(8,128)S(1)} %get-tuple-element.48), channel_id=1, source_target_pairs={{0,1},{1,0},{2,3},{3,2},{4,5},{5,4},{6,7},{7,6},{8,9},{9,8},{10,11... | collective-permute-start | bytes 786440 | tf_op jit(solution)/shard_map/ppermute | solution.py:197
  141.7 1.1 collective-permute-done.3
  142.9 22.0 %collective-permute-start.4 = (f32[64,1024]{1,0:T(8,128)S(1)}, f32[64,1024]{1,0:T(8,128)S(1)}, u32[]{:S(2)}, u32[]{:S(2)}) collective-permute-start(f32[64,1024]{1,0:T(8,128)S(1)} %get-tuple-element.58), channel_id=1, source_target_pairs={{0,8},{8,0},{1,9},{9,1},{2,10},{10,2},{3,11},{11,3},{4,12},{12,4},... | collective-permute-start | bytes 786440 | tf_op jit(solution)/shard_map/ppermute | solution.py:154
  164.9 8.2 %conditional.5 = (f32[64,1024]{1,0:T(8,128)S(1)}) conditional(s32[]{:T(128)} %bitcast.10, f32[64,1024]{1,0:T(8,128)S(1)} %get-tuple-element.57, f32[64,1024]{1,0:T(8,128)S(1)} %get-tuple-element.57), branch_computations={%region_4.5_spmd, %region_5.6_spmd} | conditional | bytes 1048584 | solution.py:199
  164.9 8.2 %all_to_all.48 = f32[4,16,1024]{2,1,0:T(8,128)S(1)} all-to-all(f32[4,16,1024]{2,1,0:T(8,128)S(1)} %copy.15), channel_id=1, replica_groups=mesh['region'=64,'zh'=2,'y'=4,'core'=2] {'y'}, dimensions={0} | all-to-all | bytes 524288 | tf_op jit(solution)/shard_map/cond/branch_1_fun/all_to_all | solution.py:157
  173.1 2.5 collective-permute-start.5
  175.7 13.3 %conditional.6 = (f32[128,1024]{1,0:T(8,128)S(1)}) conditional(s32[]{:T(128)} %bitcast.10, f32[128,1024]{1,0:T(8,128)S(1)} %get-tuple-element.50, f32[128,1024]{1,0:T(8,128)S(1)} %get-tuple-element.50), branch_computations={%region_6.7_spmd, %region_7.8_spmd} | conditional | bytes 2097160 | solution.py:202
  175.7 13.2 %all_to_all.49 = f32[8,16,1024]{2,1,0:T(8,128)S(1)} all-to-all(f32[8,16,1024]{2,1,0:T(8,128)S(1)} %copy.16), channel_id=1, replica_groups=mesh['region'=64,'zh'=2,'y'=4,'core'=2] {'y','core'}, dimensions={0} | all-to-all | bytes 1048576 | tf_op jit(solution)/shard_map/cond/branch_1_fun/all_to_all | solution.py:160
  189.0 0.0 collective-permute-done.4
  189.0 8.0 %conditional.7 = (f32[64,1024]{1,0:T(8,128)S(1)}) conditional(s32[]{:T(128)} %bitcast.10, f32[64,1024]{1,0:T(8,128)S(1)} %collective-permute-done.4, f32[64,1024]{1,0:T(8,128)S(1)} %collective-permute-done.4), branch_computations={%region_8.9_spmd, %region_9.10_spmd} | conditional | bytes 1048584 | solution.py:204
  189.0 7.9 %all_to_all.50 = f32[4,16,1024]{2,1,0:T(8,128)S(1)} all-to-all(f32[4,16,1024]{2,1,0:T(8,128)S(1)} %copy.17), channel_id=1, replica_groups=mesh['region'=64,'zh'=2,'y'=4,'core'=2] {'y'}, dimensions={0} | all-to-all | bytes 524288 | tf_op jit(solution)/shard_map/cond/branch_1_fun/all_to_all | solution.py:157
  196.9 72.6 %collective-permute-done.5.later_ref = f32[64,1024]{1,0:T(8,128)S(1)} collective-permute-done((f32[64,1024]{1,0:T(8,128)S(1)}, f32[64,1024]{1,0:T(8,128)S(1)}, u32[]{:S(2)}, u32[]{:S(2)}) %collective-permute-start.5) | collective-permute-done | bytes 262176 | tf_op jit(solution)/shard_map/ppermute | solution.py:154
  269.5 1.2 shard_map.58
  (7 shorter events, 0.2 us)
Async XLA Ops:
  0.0 41.2 %copy-start = (s32[16,1024]{1,0:T(8,128)S(1)}, s32[16,1024]{1,0:T(8,128)}, u32[]{:S(2)}) copy-start(s32[16,1024]{1,0:T(8,128)} %param.16) | copy-start | bytes 196612
  0.0 23.6 %copy-start.2 = (s32[16]{0:T(128)S(1)}, s32[16]{0:T(128)}, u32[]{:S(2)}) copy-start(s32[16]{0:T(128)} %param.17) | copy-start | bytes 196
  0.0 1.3 copy-start.1
  1.5 88.1 %collective-permute-start = (f32[128,1024]{1,0:T(8,128)S(1)}, f32[128,1024]{1,0:T(8,128)S(1)}, u32[]{:S(2)}, u32[]{:S(2)}) collective-permute-start(f32[128,1024]{1,0:T(8,128)S(1)} %get-tuple-element.39), channel_id=1, source_target_pairs={{0,8},{8,0},{1,9},{9,1},{2,10},{10,2},{3,11},{11,3},{4,12},{12,4},... | collective-permute-start | bytes 1572872 | tf_op jit(solution)/shard_map/ppermute | solution.py:154
  106.6 15.3 %collective-permute-start.1 = (f32[400,128]{1,0:T(8,128)S(1)}, f32[400,128]{1,0:T(8,128)S(1)}, u32[]{:S(2)}, u32[]{:S(2)}) collective-permute-start(f32[400,128]{1,0:T(8,128)S(1)} %get-tuple-element.44.gram_ref), channel_id=1, source_target_pairs={{0,16},{32,48},{64,80},{96,112},{128,144},{160,176},{192,208},{224... | collective-permute-start | bytes 614408 | tf_op jit(solution)/shard_map/ppermute | solution.py:166
  109.8 16.2 %collective-permute-start.2 = (f32[400,128]{1,0:T(8,128)S(1)}, f32[400,128]{1,0:T(8,128)S(1)}, u32[]{:S(2)}, u32[]{:S(2)}) collective-permute-start(f32[400,128]{1,0:T(8,128)S(1)} %get-tuple-element.44.gram_ref), channel_id=1, source_target_pairs={{16,32},{48,64},{80,96},{112,128},{144,160},{176,192},{208,224},{2... | collective-permute-start | bytes 614408 | tf_op jit(solution)/shard_map/ppermute | solution.py:166
  137.8 5.0 %collective-permute-start.3 = (f32[64,1024]{1,0:T(8,128)S(1)}, f32[64,1024]{1,0:T(8,128)S(1)}, u32[]{:S(2)}, u32[]{:S(2)}) collective-permute-start(f32[64,1024]{1,0:T(8,128)S(1)} %get-tuple-element.48), channel_id=1, source_target_pairs={{0,1},{1,0},{2,3},{3,2},{4,5},{5,4},{6,7},{7,6},{8,9},{9,8},{10,11... | collective-permute-start | bytes 786440 | tf_op jit(solution)/shard_map/ppermute | solution.py:197
  142.9 46.1 %collective-permute-start.4 = (f32[64,1024]{1,0:T(8,128)S(1)}, f32[64,1024]{1,0:T(8,128)S(1)}, u32[]{:S(2)}, u32[]{:S(2)}) collective-permute-start(f32[64,1024]{1,0:T(8,128)S(1)} %get-tuple-element.58), channel_id=1, source_target_pairs={{0,8},{8,0},{1,9},{9,1},{2,10},{10,2},{3,11},{11,3},{4,12},{12,4},... | collective-permute-start | bytes 786440 | tf_op jit(solution)/shard_map/ppermute | solution.py:154
  173.1 96.4 %collective-permute-start.5 = (f32[64,1024]{1,0:T(8,128)S(1)}, f32[64,1024]{1,0:T(8,128)S(1)}, u32[]{:S(2)}, u32[]{:S(2)}) collective-permute-start(f32[64,1024]{1,0:T(8,128)S(1)} %get-tuple-element.64), channel_id=1, source_target_pairs={{0,8},{8,0},{1,9},{9,1},{2,10},{10,2},{3,11},{11,3},{4,12},{12,4},... | collective-permute-start | bytes 786440 | tf_op jit(solution)/shard_map/ppermute | solution.py:154
